TPU v7x, 128 devices: a whole 4x4x4 slice. The times are simulated.
128 devices in a mesh: det: 16 (over x_hi, z, core), frames: 8 (over y, x_lo).
Axes of the slice: x: 4 (x_hi: 2, x_lo: 2; x = x_hi * 2 + x_lo), y: 4, z: 4, core: 2. Of those that a mesh axis runs over, the one named last changes fastest.
Arguments:
- probe: bfloat16 [2, 2048, 2048], P(None, 'det'), may hold values from -6 to 6
- object_field: bfloat16 [2, 2048, 2304], P(None, 'det'), may hold values from -4 to 4
- positions: int32 [8], P('frames'), may hold values from 0 to 256, as said below
- cotangent: bfloat16 [8, 2048, 2048], P('frames', 'det'), may hold values from -6 to 6
- kernel: float32 [57, 57], replicated, may hold values from 0 to 0.03508772
Outputs:
- wave_grad: bfloat16 [2, 8, 2048, 2048], P(None, 'frames', 'det')
- kernel_grad: float32 [57, 57], replicated
Inputs may be any that keep to these rules, and one draw needn't show every extreme that they name: positions[f] is the first object column of frame f's window; some frame starts at 0 and some at 256.
All inputs are finite; a program needn't handle non-finite values.
Results may differ from a plain program's by a relative error of at most 0.011.
Values may be sent and summed in bfloat16 or wider, within the bound.
A program may use at most 128 MiB of HBM per device.

v0:
```python
import math

import jax
import jax.numpy as jnp
from jax import lax
from jax.sharding import PartitionSpec as P


def extended_2(block, sides, width):
    for axis, dim in sides:
        count = lax.axis_size(axis)
        forward = [(i, i + 1) for i in range(count - 1)]
        forward.append((count - 1, 0))
        backward = [(target, source) for source, target in forward]
        low = lax.ppermute(
            lax.slice_in_dim(block, block.shape[dim] - width, None, axis=dim), axis, forward
        )
        high = lax.ppermute(lax.slice_in_dim(block, 0, width, axis=dim), axis, backward)
        block = jnp.concatenate([low, block, high], axis=dim)
    return block


def dft_tables(extent):
    block_width = min(128, extent)
    table_scale = 1.0 / math.sqrt(extent)
    columns = jnp.arange(extent, dtype=jnp.int32)

    def one_block(row_index):
        product = row_index[:, None] * columns[None, :] % extent
        phase_angle = product.astype(jnp.float32) * (2.0 * math.pi / extent)
        cosine = (jnp.cos(phase_angle) * table_scale).astype(jnp.bfloat16)
        sine = (jnp.sin(phase_angle) * table_scale).astype(jnp.bfloat16)
        return (cosine, sine)

    row_blocks = jnp.arange(extent, dtype=jnp.int32).reshape(extent // block_width, block_width)
    cosine, sine = lax.map(one_block, row_blocks)
    return (cosine.reshape(extent, extent), sine.reshape(extent, extent))


def band_stack(kernel, width):
    tap_count = kernel.shape[0]
    kernel_reach = tap_count - 1
    outer_index = jnp.arange(width + kernel_reach, dtype=jnp.int32)
    inner_index = jnp.arange(width, dtype=jnp.int32)
    lag_index = jnp.arange(tap_count, dtype=jnp.int32)
    band_marks = (
        outer_index[:, None, None] - inner_index[None, :, None] == lag_index[None, None, :]
    ).astype(jnp.float32)
    rounded = lax.optimization_barrier(kernel.astype(jnp.bfloat16)).astype(jnp.float32)
    across = jnp.einsum("ij,zyj->izy", rounded, band_marks, precision=lax.Precision.HIGHEST).astype(
        jnp.bfloat16
    )
    downward = jnp.einsum(
        "ij,zyi->jyz", rounded, band_marks, precision=lax.Precision.HIGHEST
    ).astype(jnp.bfloat16)
    return (across, downward)


def band_sums(products, tap_count):
    group_size, local_rows, extent = products.shape
    flattened = products.reshape(group_size, local_rows * extent)
    flattened = jnp.pad(flattened, ((0, 0), (0, local_rows)))
    skewed = flattened.reshape(group_size, local_rows, extent + 1)
    return jnp.sum(skewed[:, :, :tap_count], axis=1)


def right_product(values, table):
    return jnp.einsum("frn,nl->frl", values, table, preferred_element_type=jnp.float32)


def left_product(table, values):
    return jnp.einsum("km,fmr->fkr", table, values, preferred_element_type=jnp.float32)


def detector_side(intensity_rows, extended, downward):
    tap_count = downward.shape[0]
    kernel_reach = (tap_count - 1) // 2
    extent = extended.shape[2]
    padded = jnp.concatenate(
        [extended[:, :, extent - kernel_reach :], extended, extended[:, :, :kernel_reach]], axis=2
    )

    def turn(group_index, carried):
        gradient, lag_sums = carried
        first_tap = group_index * 3
        shifted = jnp.stack(
            [
                lax.dynamic_slice_in_dim(padded, first_tap + tap_offset, extent, 2)
                for tap_offset in range(3)
            ]
        )
        weights = lax.dynamic_slice_in_dim(downward, first_tap, 3, 0)
        gradient = gradient + jnp.einsum(
            "syz,sfzn->fyn", weights, shifted, preferred_element_type=jnp.float32
        )
        products = jnp.einsum(
            "fyn,sfzn->syz", intensity_rows, shifted, preferred_element_type=jnp.float32
        )
        lag_sums = lax.dynamic_update_slice_in_dim(
            lag_sums, band_sums(products, tap_count), first_tap, 0
        )
        return (gradient, lag_sums)

    start_value = (
        jnp.zeros(intensity_rows.shape, jnp.float32),
        jnp.zeros((tap_count, tap_count), jnp.float32),
    )
    gradient, lag_sums = lax.fori_loop(0, tap_count // 3, turn, start_value)
    return (gradient, jnp.transpose(lag_sums))


def on_device(probe, object_field, positions, cotangent, kernel):
    extent = probe.shape[2]
    local_rows = probe.shape[1]
    kernel_reach = (kernel.shape[0] - 1) // 2
    cosine, sine = dft_tables(extent)
    window = jax.vmap(
        lambda column_start: lax.dynamic_slice_in_dim(object_field, column_start, extent, 2),
        out_axes=1,
    )(positions)
    probe_re = probe[0].astype(jnp.float32)
    probe_im = probe[1].astype(jnp.float32)
    window_re = window[0].astype(jnp.float32)
    window_im = window[1].astype(jnp.float32)
    wave_re = (probe_re * window_re - probe_im * window_im).astype(jnp.bfloat16)
    wave_im = (probe_re * window_im + probe_im * window_re).astype(jnp.bfloat16)
    half_transform = jnp.stack(
        [
            right_product(wave_re, cosine) + right_product(wave_im, sine),
            right_product(wave_im, cosine) - right_product(wave_re, sine),
        ]
    ).astype(jnp.bfloat16)
    received = lax.all_to_all(half_transform, "det", split_axis=3, concat_axis=2, tiled=True)
    spectrum = jnp.stack(
        [
            left_product(cosine, received[0]) + left_product(sine, received[1]),
            left_product(cosine, received[1]) - left_product(sine, received[0]),
        ]
    )
    intensity = (spectrum[0] * spectrum[0] + spectrum[1] * spectrum[1]).astype(jnp.bfloat16)
    across, downward = band_stack(kernel, local_rows)
    intensity_rows = lax.all_to_all(intensity, "det", split_axis=1, concat_axis=2, tiled=True)
    extended = extended_2(cotangent, (("det", 1),), kernel_reach)
    gradient, lag_sums = detector_side(intensity_rows, extended, downward)
    gradient_cols = lax.all_to_all(
        gradient.astype(jnp.bfloat16), "det", split_axis=2, concat_axis=1, tiled=True
    )
    grad_wide = gradient_cols.astype(jnp.float32)
    weight_re = (2.0 * grad_wide * spectrum[0]).astype(jnp.bfloat16)
    weight_im = (2.0 * grad_wide * spectrum[1]).astype(jnp.bfloat16)
    back_transform = jnp.stack(
        [
            left_product(cosine, weight_re) - left_product(sine, weight_im),
            left_product(cosine, weight_im) + left_product(sine, weight_re),
        ]
    ).astype(jnp.bfloat16)
    received = lax.all_to_all(back_transform, "det", split_axis=2, concat_axis=3, tiled=True)
    wave_grad = jnp.stack(
        [
            right_product(received[0], cosine) - right_product(received[1], sine),
            right_product(received[1], cosine) + right_product(received[0], sine),
        ]
    ).astype(jnp.bfloat16)
    frames_total = positions.shape[0] * lax.axis_size("frames")
    kernel_grad = lax.psum(lag_sums, ("det", "frames")) / (frames_total * extent)
    return (wave_grad, kernel_grad)


def solution(mesh):
    placed = (
        P(None, "det", None),
        P(None, "det", None),
        P("frames"),
        P("frames", "det", None),
        P(),
    )
    return jax.shard_map(
        on_device,
        mesh=mesh,
        in_specs=placed,
        out_specs=(P(None, "frames", "det", None), P()),
        check_vma=False,
    )
```

profile of v0, /device:TPU:1, one launch (start us, length us, event | category | flops | bytes accessed | tf_op | source)
XLA Modules:
  0.0 514.9 jit_solution(13225017239695306538)
XLA Ops:
  0.7 90.8 %while.34 = (s32[]{:T(128)}, bf16[16,128,2048]{2,1,0:T(8,128)(2,1)}, bf16[16,128,2048]{2,1,0:T(8,128)(2,1)}, s32[16,128]{1,0:T(8,128)S(1)}, s32[]{:T(128)}) while((s32[]{:T(128)}, bf16[16,128,2048]{2,1,0:T(8,128)(2,1)}, bf16[16,128,2048]{2,1,0:T(8,128)(2,1)}, s32[16,128]{1,0:T(8,128)S(1)}, s32[]{:T(128)}) %tuple.93), condition=%wide.region_1.2_spmd.clone, body=%wide.region_0.1_spmd.clone.sunk | while | flops 4718594 | bytes 1050689 | solution.py:36
  0.7 5.7 %fusion.92 = (bf16[16,128,2048]{2,1,0:T(8,128)(2,1)}, bf16[16,128,2048]{2,1,0:T(8,128)(2,1)}) fusion(bf16[16,128,2048]{2,1,0:T(8,128)(2,1)} %get-tuple-element.426, s32[]{:T(128)} %get-tuple-element.424, s32[128]{0:T(128)S(1)} %fusion.91, bf16[16,128,2048]{2,1,0:T(8,128)(2,1)} %get-tuple-element.425), kind=kLoop, calls=%fused_computation.14.clone.1 | loop fusion | flops 4718592 | bytes 1049600 | tf_op jit(solution)/shard_map/while/body/jit(dynamic_update_index_in_dim)/dynamic_update_slice | solution.py:36
  6.4 5.7 %fusion.92 = (bf16[16,128,2048]{2,1,0:T(8,128)(2,1)}, bf16[16,128,2048]{2,1,0:T(8,128)(2,1)}) fusion(bf16[16,128,2048]{2,1,0:T(8,128)(2,1)} %get-tuple-element.426, s32[]{:T(128)} %get-tuple-element.424, s32[128]{0:T(128)S(1)} %fusion.91, bf16[16,128,2048]{2,1,0:T(8,128)(2,1)} %get-tuple-element.425), kind=kLoop, calls=%fused_computation.14.clone.1 | loop fusion | flops 4718592 | bytes 1049600 | tf_op jit(solution)/shard_map/while/body/jit(dynamic_update_index_in_dim)/dynamic_update_slice | solution.py:36
  12.1 5.7 %fusion.92 = (bf16[16,128,2048]{2,1,0:T(8,128)(2,1)}, bf16[16,128,2048]{2,1,0:T(8,128)(2,1)}) fusion(bf16[16,128,2048]{2,1,0:T(8,128)(2,1)} %get-tuple-element.426, s32[]{:T(128)} %get-tuple-element.424, s32[128]{0:T(128)S(1)} %fusion.91, bf16[16,128,2048]{2,1,0:T(8,128)(2,1)} %get-tuple-element.425), kind=kLoop, calls=%fused_computation.14.clone.1 | loop fusion | flops 4718592 | bytes 1049600 | tf_op jit(solution)/shard_map/while/body/jit(dynamic_update_index_in_dim)/dynamic_update_slice | solution.py:36
  17.7 5.7 %fusion.92 = (bf16[16,128,2048]{2,1,0:T(8,128)(2,1)}, bf16[16,128,2048]{2,1,0:T(8,128)(2,1)}) fusion(bf16[16,128,2048]{2,1,0:T(8,128)(2,1)} %get-tuple-element.426, s32[]{:T(128)} %get-tuple-element.424, s32[128]{0:T(128)S(1)} %fusion.91, bf16[16,128,2048]{2,1,0:T(8,128)(2,1)} %get-tuple-element.425), kind=kLoop, calls=%fused_computation.14.clone.1 | loop fusion | flops 4718592 | bytes 1049600 | tf_op jit(solution)/shard_map/while/body/jit(dynamic_update_index_in_dim)/dynamic_update_slice | solution.py:36
  23.4 5.7 %fusion.92 = (bf16[16,128,2048]{2,1,0:T(8,128)(2,1)}, bf16[16,128,2048]{2,1,0:T(8,128)(2,1)}) fusion(bf16[16,128,2048]{2,1,0:T(8,128)(2,1)} %get-tuple-element.426, s32[]{:T(128)} %get-tuple-element.424, s32[128]{0:T(128)S(1)} %fusion.91, bf16[16,128,2048]{2,1,0:T(8,128)(2,1)} %get-tuple-element.425), kind=kLoop, calls=%fused_computation.14.clone.1 | loop fusion | flops 4718592 | bytes 1049600 | tf_op jit(solution)/shard_map/while/body/jit(dynamic_update_index_in_dim)/dynamic_update_slice | solution.py:36
  29.1 5.7 %fusion.92 = (bf16[16,128,2048]{2,1,0:T(8,128)(2,1)}, bf16[16,128,2048]{2,1,0:T(8,128)(2,1)}) fusion(bf16[16,128,2048]{2,1,0:T(8,128)(2,1)} %get-tuple-element.426, s32[]{:T(128)} %get-tuple-element.424, s32[128]{0:T(128)S(1)} %fusion.91, bf16[16,128,2048]{2,1,0:T(8,128)(2,1)} %get-tuple-element.425), kind=kLoop, calls=%fused_computation.14.clone.1 | loop fusion | flops 4718592 | bytes 1049600 | tf_op jit(solution)/shard_map/while/body/jit(dynamic_update_index_in_dim)/dynamic_update_slice | solution.py:36
  34.7 5.7 %fusion.92 = (bf16[16,128,2048]{2,1,0:T(8,128)(2,1)}, bf16[16,128,2048]{2,1,0:T(8,128)(2,1)}) fusion(bf16[16,128,2048]{2,1,0:T(8,128)(2,1)} %get-tuple-element.426, s32[]{:T(128)} %get-tuple-element.424, s32[128]{0:T(128)S(1)} %fusion.91, bf16[16,128,2048]{2,1,0:T(8,128)(2,1)} %get-tuple-element.425), kind=kLoop, calls=%fused_computation.14.clone.1 | loop fusion | flops 4718592 | bytes 1049600 | tf_op jit(solution)/shard_map/while/body/jit(dynamic_update_index_in_dim)/dynamic_update_slice | solution.py:36
  40.4 5.7 %fusion.92 = (bf16[16,128,2048]{2,1,0:T(8,128)(2,1)}, bf16[16,128,2048]{2,1,0:T(8,128)(2,1)}) fusion(bf16[16,128,2048]{2,1,0:T(8,128)(2,1)} %get-tuple-element.426, s32[]{:T(128)} %get-tuple-element.424, s32[128]{0:T(128)S(1)} %fusion.91, bf16[16,128,2048]{2,1,0:T(8,128)(2,1)} %get-tuple-element.425), kind=kLoop, calls=%fused_computation.14.clone.1 | loop fusion | flops 4718592 | bytes 1049600 | tf_op jit(solution)/shard_map/while/body/jit(dynamic_update_index_in_dim)/dynamic_update_slice | solution.py:36
  46.1 5.7 %fusion.92 = (bf16[16,128,2048]{2,1,0:T(8,128)(2,1)}, bf16[16,128,2048]{2,1,0:T(8,128)(2,1)}) fusion(bf16[16,128,2048]{2,1,0:T(8,128)(2,1)} %get-tuple-element.426, s32[]{:T(128)} %get-tuple-element.424, s32[128]{0:T(128)S(1)} %fusion.91, bf16[16,128,2048]{2,1,0:T(8,128)(2,1)} %get-tuple-element.425), kind=kLoop, calls=%fused_computation.14.clone.1 | loop fusion | flops 4718592 | bytes 1049600 | tf_op jit(solution)/shard_map/while/body/jit(dynamic_update_index_in_dim)/dynamic_update_slice | solution.py:36
  51.8 5.7 %fusion.92 = (bf16[16,128,2048]{2,1,0:T(8,128)(2,1)}, bf16[16,128,2048]{2,1,0:T(8,128)(2,1)}) fusion(bf16[16,128,2048]{2,1,0:T(8,128)(2,1)} %get-tuple-element.426, s32[]{:T(128)} %get-tuple-element.424, s32[128]{0:T(128)S(1)} %fusion.91, bf16[16,128,2048]{2,1,0:T(8,128)(2,1)} %get-tuple-element.425), kind=kLoop, calls=%fused_computation.14.clone.1 | loop fusion | flops 4718592 | bytes 1049600 | tf_op jit(solution)/shard_map/while/body/jit(dynamic_update_index_in_dim)/dynamic_update_slice | solution.py:36
  57.5 5.7 %fusion.92 = (bf16[16,128,2048]{2,1,0:T(8,128)(2,1)}, bf16[16,128,2048]{2,1,0:T(8,128)(2,1)}) fusion(bf16[16,128,2048]{2,1,0:T(8,128)(2,1)} %get-tuple-element.426, s32[]{:T(128)} %get-tuple-element.424, s32[128]{0:T(128)S(1)} %fusion.91, bf16[16,128,2048]{2,1,0:T(8,128)(2,1)} %get-tuple-element.425), kind=kLoop, calls=%fused_computation.14.clone.1 | loop fusion | flops 4718592 | bytes 1049600 | tf_op jit(solution)/shard_map/while/body/jit(dynamic_update_index_in_dim)/dynamic_update_slice | solution.py:36
  63.2 5.7 %fusion.92 = (bf16[16,128,2048]{2,1,0:T(8,128)(2,1)}, bf16[16,128,2048]{2,1,0:T(8,128)(2,1)}) fusion(bf16[16,128,2048]{2,1,0:T(8,128)(2,1)} %get-tuple-element.426, s32[]{:T(128)} %get-tuple-element.424, s32[128]{0:T(128)S(1)} %fusion.91, bf16[16,128,2048]{2,1,0:T(8,128)(2,1)} %get-tuple-element.425), kind=kLoop, calls=%fused_computation.14.clone.1 | loop fusion | flops 4718592 | bytes 1049600 | tf_op jit(solution)/shard_map/while/body/jit(dynamic_update_index_in_dim)/dynamic_update_slice | solution.py:36
  68.8 5.7 %fusion.92 = (bf16[16,128,2048]{2,1,0:T(8,128)(2,1)}, bf16[16,128,2048]{2,1,0:T(8,128)(2,1)}) fusion(bf16[16,128,2048]{2,1,0:T(8,128)(2,1)} %get-tuple-element.426, s32[]{:T(128)} %get-tuple-element.424, s32[128]{0:T(128)S(1)} %fusion.91, bf16[16,128,2048]{2,1,0:T(8,128)(2,1)} %get-tuple-element.425), kind=kLoop, calls=%fused_computation.14.clone.1 | loop fusion | flops 4718592 | bytes 1049600 | tf_op jit(solution)/shard_map/while/body/jit(dynamic_update_index_in_dim)/dynamic_update_slice | solution.py:36
  74.5 5.7 %fusion.92 = (bf16[16,128,2048]{2,1,0:T(8,128)(2,1)}, bf16[16,128,2048]{2,1,0:T(8,128)(2,1)}) fusion(bf16[16,128,2048]{2,1,0:T(8,128)(2,1)} %get-tuple-element.426, s32[]{:T(128)} %get-tuple-element.424, s32[128]{0:T(128)S(1)} %fusion.91, bf16[16,128,2048]{2,1,0:T(8,128)(2,1)} %get-tuple-element.425), kind=kLoop, calls=%fused_computation.14.clone.1 | loop fusion | flops 4718592 | bytes 1049600 | tf_op jit(solution)/shard_map/while/body/jit(dynamic_update_index_in_dim)/dynamic_update_slice | solution.py:36
  80.2 5.7 %fusion.92 = (bf16[16,128,2048]{2,1,0:T(8,128)(2,1)}, bf16[16,128,2048]{2,1,0:T(8,128)(2,1)}) fusion(bf16[16,128,2048]{2,1,0:T(8,128)(2,1)} %get-tuple-element.426, s32[]{:T(128)} %get-tuple-element.424, s32[128]{0:T(128)S(1)} %fusion.91, bf16[16,128,2048]{2,1,0:T(8,128)(2,1)} %get-tuple-element.425), kind=kLoop, calls=%fused_computation.14.clone.1 | loop fusion | flops 4718592 | bytes 1049600 | tf_op jit(solution)/shard_map/while/body/jit(dynamic_update_index_in_dim)/dynamic_update_slice | solution.py:36
  85.8 5.7 %fusion.92 = (bf16[16,128,2048]{2,1,0:T(8,128)(2,1)}, bf16[16,128,2048]{2,1,0:T(8,128)(2,1)}) fusion(bf16[16,128,2048]{2,1,0:T(8,128)(2,1)} %get-tuple-element.426, s32[]{:T(128)} %get-tuple-element.424, s32[128]{0:T(128)S(1)} %fusion.91, bf16[16,128,2048]{2,1,0:T(8,128)(2,1)} %get-tuple-element.425), kind=kLoop, calls=%fused_computation.14.clone.1 | loop fusion | flops 4718592 | bytes 1049600 | tf_op jit(solution)/shard_map/while/body/jit(dynamic_update_index_in_dim)/dynamic_update_slice | solution.py:36
  94.2 4.8 fusion.46
  105.4 2.0 copy.64
  107.4 9.3 %all-to-all-start = ((bf16[2,1,128,2048]{2,0,1,3:T(2,128)(2,1)}), bf16[2,1,128,2048]{2,0,1,3:T(2,128)(2,1)S(1)}, u32[]{:S(2)}, u32[]{:S(2)}) async-start(bf16[2,1,128,2048]{2,0,1,3:T(2,128)(2,1)} %copy.64), calls=%async_computation | async-start | bytes 2097152 | tf_op jit(solution)/shard_map/all_to_all | solution.py:133
  119.7 14.3 %all-to-all-done = bf16[2,1,128,2048]{2,0,1,3:T(2,128)(2,1)S(1)} async-done(((bf16[2,1,128,2048]{2,0,1,3:T(2,128)(2,1)}), bf16[2,1,128,2048]{2,0,1,3:T(2,128)(2,1)S(1)}, u32[]{:S(2)}, u32[]{:S(2)}) %all-to-all-start) | async-done | bytes 1048608 | tf_op jit(solution)/shard_map/all_to_all | solution.py:133
  134.4 6.3 %fusion.48 = f32[128,2048]{1,0:T(8,128)S(1)} fusion(bf16[2048,128]{1,0:T(8,128)(2,1)S(1)} %bitcast.191, bf16[2048,2048]{1,0:T(8,128)(2,1)} %bitcast.178), kind=kOutput, calls=%fused_computation.91 | convolution fusion | flops 1073741824 | bytes 9961472 | tf_op jit(solution)/shard_map/km,fmr->fkr/dot_general | solution.py:72
  141.1 6.5 %fusion.49 = f32[128,2048]{1,0:T(8,128)S(1)} fusion(bf16[2048,128]{1,0:T(8,128)(2,1)S(1)} %bitcast.193, bf16[2048,2048]{1,0:T(8,128)(2,1)} %bitcast.179), kind=kOutput, calls=%fused_computation.92 | convolution fusion | flops 1073741824 | bytes 9961472 | tf_op jit(solution)/shard_map/km,fmr->fkr/dot_general | solution.py:72
  147.5 6.4 %fusion.20 = f32[1,2048,128]{1,2,0:T(8,128)S(1)} fusion(f32[128,2048]{1,0:T(8,128)S(1)} %fusion.48, bf16[2048,128]{1,0:T(8,128)(2,1)S(1)} %bitcast.194, bf16[2048,2048]{1,0:T(8,128)(2,1)} %bitcast.161), kind=kOutput, calls=%fused_computation.41 | convolution fusion | flops 1074003968 | bytes 11010048 | tf_op jit(solution)/shard_map/km,fmr->fkr/dot_general | solution.py:72
  154.0 3.9 add_convert_fusion
  159.4 11.5 %reduce = bf16[2048,128]{1,0:T(8,128)(2,1)S(1)} reduce(bf16[2048,1,128]{2,1,0:T(2,128)(2,1)S(1)} %bitcast.197, bf16[]{:T(256)} %broadcast.291), dimensions={1}, to_apply=%bitcast.107.reduce_sub_computation | reduce | bytes 1048578
  171.8 5.0 all-to-all-start.1
  176.9 3.4 convert_bitcast_fusion
  180.3 5.1 copy.70
  190.1 162.2 %while.35 = (s32[]{:T(128)}, f32[1,128,2048]{1,2,0:T(8,128)}, f32[57,57]{1,0:T(8,128)S(1)}, bf16[1,184,2104]{2,1,0:T(8,128)(2,1)S(1)}, bf16[57,128,184]{1,2,0:T(...) while((s32[]{:T(128)}, f32[1,128,2048]{1,2,0:T(8,128)}, ...), condition=%wide.region_4.5_spmd.clone, body=%wide.region_2.4_spmd.clone.sunk | while | flops 583881920 | bytes 17459568 | solution.py:108
  192.0 1.8 convolution_bitcast_fusion.3
  195.2 3.0 fusion.95
  203.4 3.4 fusion.95
  212.0 3.4 fusion.95
  220.5 3.4 fusion.95
  229.1 3.4 fusion.95
  237.6 3.4 fusion.95
  246.2 3.4 fusion.95
  254.8 3.4 fusion.95
  263.3 3.4 fusion.95
  271.9 3.4 fusion.95
  280.4 3.4 fusion.95
  289.0 3.4 fusion.95
  297.5 3.4 fusion.95
  306.1 3.4 fusion.95
  314.6 3.4 fusion.95
  323.2 3.4 fusion.95
  331.8 3.4 fusion.95
  340.3 3.4 fusion.95
  348.9 3.4 fusion.95
  353.7 8.4 %copy.85 = bf16[1,128,2048]{1,0,2:T(2,128)(2,1)S(1)} copy(bf16[1,128,2048]{1,2,0:T(8,128)(2,1)S(1)} %convert_element_type.180) | data formatting | bytes 1048576 | tf_op jit(solution)/shard_map/convert_element_type | solution.py:146
  362.1 12.2 %reduce.1 = bf16[2048,128]{1,0:T(8,128)(2,1)} reduce(bf16[2048,1,128]{2,1,0:T(2,128)(2,1)S(1)} %bitcast.199, bf16[]{:T(256)} %broadcast.291), dimensions={1}, to_apply=%bitcast.146.reduce_sub_computation | reduce | bytes 1048578
  375.5 17.8 %all_to_all.57 = bf16[16,2,8192]{2,1,0:T(2,128)(2,1)} all-to-all(bf16[16,2,8192]{2,1,0:T(2,128)(2,1)S(1)} %reshape.540), channel_id=1, replica_groups=mesh['det'=16,'frames'=8] {'det'}, dimensions={0} | all-to-all | bytes 1048576 | tf_op jit(solution)/shard_map/all_to_all | solution.py:145
  393.3 2.2 reshape.541
  399.9 6.4 %fusion.50 = f32[128,2048]{1,0:T(8,128)S(1)} fusion(bf16[2048,128]{0,1:T(8,128)(2,1)S(1)} %get-tuple-element.337, bf16[2048,2048]{1,0:T(8,128)(2,1)} %bitcast.180), kind=kOutput, calls=%fused_computation.93 | convolution fusion | flops 1073741824 | bytes 9961472 | tf_op jit(solution)/shard_map/km,fmr->fkr/dot_general | solution.py:72
  406.3 6.4 %fusion.51 = f32[128,2048]{1,0:T(8,128)S(1)} fusion(bf16[2048,128]{0,1:T(8,128)(2,1)S(1)} %get-tuple-element.338, bf16[2048,2048]{1,0:T(8,128)(2,1)} %bitcast.181), kind=kOutput, calls=%fused_computation.94 | convolution fusion | flops 1073741824 | bytes 9961472 | tf_op jit(solution)/shard_map/km,fmr->fkr/dot_general | solution.py:72
  412.8 2.9 fusion.30
  415.7 2.9 fusion.29
  418.7 2.0 copy.74
  420.7 4.6 all-to-all-start.3
  425.4 71.2 %psum.7 = f32[57,57]{1,0:T(8,128)S(1)} all-reduce(f32[57,57]{1,0:T(8,128)S(1)} %bitcast.204), channel_id=1, replica_groups=mesh['det'=16,'frames'=8] {'det','frames'}, use_global_device_ids=true, to_apply=%region_5.6 | all-reduce | flops 3249 | bytes 25992 | tf_op jit(solution)/shard_map/psum | solution.py:165
  497.7 4.7 fusion.52
  502.7 4.8 fusion.53
  507.5 4.8 fusion.28
  (295 shorter events, 125.0 us)
Async XLA Ops:
  0.6 91.5 %copy-start = (bf16[2,128,2304]{2,1,0:T(8,128)(2,1)S(1)}, bf16[2,128,2304]{2,1,0:T(8,128)(2,1)}, u32[]{:S(2)}) copy-start(bf16[2,128,2304]{2,1,0:T(8,128)(2,1)} %param.10) | copy-start | bytes 3538948
  94.2 4.8 slice-start.8
  94.2 5.8 %slice-start.9 = ((s8[8388608]{0:T(1024)(128)(4,1)}), s8[4194304]{0:T(1024)(128)(4,1)S(1)}, s32[]{:S(2)}) async-start(s8[8388608]{0:T(1024)(128)(4,1)} %bitcast.184), calls=%async_computation.13 | async-start | bytes 8388608
  99.0 2.5 slice-start
  100.1 2.6 slice-start.1
  104.0 12.8 %copy-start.6 = (bf16[1,128,2048]{2,1,0:T(8,128)(2,1)S(1)}, bf16[1,128,2048]{2,1,0:T(8,128)(2,1)}, u32[]{:S(2)}) copy-start(bf16[1,128,2048]{2,1,0:T(8,128)(2,1)} %param.12) | copy-start | bytes 1572868
  104.0 15.6 %copy-start.8 = (f32[57,57]{1,0:T(8,128)S(1)}, f32[57,57]{1,0:T(8,128)}, u32[]{:S(2)}) copy-start(f32[57,57]{1,0:T(8,128)} %param.13) | copy-start | bytes 38992
  107.4 26.5 %all-to-all-start = ((bf16[2,1,128,2048]{2,0,1,3:T(2,128)(2,1)}), bf16[2,1,128,2048]{2,0,1,3:T(2,128)(2,1)S(1)}, u32[]{:S(2)}, u32[]{:S(2)}) async-start(bf16[2,1,128,2048]{2,0,1,3:T(2,128)(2,1)} %copy.64), calls=%async_computation | async-start | bytes 2097152 | tf_op jit(solution)/shard_map/all_to_all | solution.py:133
  117.5 67.9 %collective-permute-start = (bf16[1,28,2048]{2,1,0:T(8,128)(2,1)}, bf16[1,28,2048]{2,1,0:T(8,128)(2,1)S(1)}, u32[]{:S(2)}, u32[]{:S(2)}) collective-permute-start(bf16[1,28,2048]{2,1,0:T(8,128)(2,1)} %get-tuple-element.343), channel_id=1, source_target_pairs={{0,8},{8,16},{16,24},{24,32},{32,40},{40,48},{48,56},{56,64},{64,7... | collective-permute-start | bytes 344072 | tf_op jit(solution)/shard_map/ppermute | solution.py:15
  119.1 66.3 %collective-permute-start.1 = (bf16[1,28,2048]{2,1,0:T(8,128)(2,1)}, bf16[1,28,2048]{2,1,0:T(8,128)(2,1)S(1)}, u32[]{:S(2)}, u32[]{:S(2)}) collective-permute-start(bf16[1,28,2048]{2,1,0:T(8,128)(2,1)} %get-tuple-element.344), channel_id=1, source_target_pairs={{8,0},{16,8},{24,16},{32,24},{40,32},{48,40},{56,48},{64,56},{72,6... | collective-permute-start | bytes 344072 | tf_op jit(solution)/shard_map/ppermute | solution.py:18
  141.0 12.9 %slice-start.2 = ((s8[8388608]{0:T(1024)(128)(4,1)}), s8[4194304]{0:T(1024)(128)(4,1)S(1)}, s32[]{:S(2)}) async-start(s8[8388608]{0:T(1024)(128)(4,1)} %bitcast.167), calls=%async_computation.6 | async-start | bytes 8388608
  147.5 6.5 %slice-start.3 = ((s8[8388608]{0:T(1024)(128)(4,1)}), s8[4194304]{0:T(1024)(128)(4,1)S(1)}, s32[]{:S(2)}) async-start(s8[8388608]{0:T(1024)(128)(4,1)} %bitcast.167), calls=%async_computation.7 | async-start | bytes 8388608
  154.0 17.8 %copy-start.3 = (f32[1,2048,128]{1,2,0:T(8,128)}, f32[1,2048,128]{1,2,0:T(8,128)S(1)}, u32[]{:S(2)}) copy-start(f32[1,2048,128]{1,2,0:T(8,128)S(1)} %fusion.20) | copy-start | bytes 3145732
  157.9 27.5 %copy-start.7 = (bf16[1,128,2048]{2,1,0:T(8,128)(2,1)S(1)}, bf16[1,128,2048]{2,1,0:T(8,128)(2,1)}, u32[]{:S(2)}) copy-start(bf16[1,128,2048]{2,1,0:T(8,128)(2,1)} %param.12) | copy-start | bytes 1572868
  171.8 16.3 %all-to-all-start.1 = ((bf16[16,2,8192]{2,1,0:T(2,128)(2,1)}), bf16[16,2,8192]{2,1,0:T(2,128)(2,1)S(1)}, u32[]{:S(2)}, u32[]{:S(2)}) async-start(bf16[16,2,8192]{2,1,0:T(2,128)(2,1)} %reshape.538), calls=%async_computation.1 | async-start | bytes 1048576 | tf_op jit(solution)/shard_map/all_to_all | solution.py:142
  191.1 0.9 copy-start.2
  199.3 0.9 copy-start.2
  207.9 0.9 copy-start.2
  216.5 0.9 copy-start.2
  225.0 0.9 copy-start.2
  233.6 0.9 copy-start.2
  242.1 0.9 copy-start.2
  250.7 0.9 copy-start.2
  259.2 0.9 copy-start.2
  267.8 0.9 copy-start.2
  276.3 0.9 copy-start.2
  284.9 0.9 copy-start.2
  293.5 0.9 copy-start.2
  302.0 0.9 copy-start.2
  310.6 0.9 copy-start.2
  319.1 0.9 copy-start.2
  327.7 0.9 copy-start.2
  336.2 0.9 copy-start.2
  344.8 0.9 copy-start.2
  352.3 46.2 %copy-start.4 = (f32[1,2048,128]{1,2,0:T(8,128)S(1)}, f32[1,2048,128]{1,2,0:T(8,128)}, u32[]{:S(2)}) copy-start(f32[1,2048,128]{1,2,0:T(8,128)} %copy-done.3) | copy-start | bytes 3145732
  352.3 46.2 %copy-start.5 = (f32[1,2048,128]{1,2,0:T(8,128)S(1)}, f32[1,2048,128]{1,2,0:T(8,128)}, u32[]{:S(2)}) copy-start(f32[1,2048,128]{1,2,0:T(8,128)} %get-tuple-element.346) | copy-start | bytes 3145732
  399.9 12.9 %slice-start.4 = ((s8[8388608]{0:T(1024)(128)(4,1)}), s8[4194304]{0:T(1024)(128)(4,1)S(1)}, s32[]{:S(2)}) async-start(s8[8388608]{0:T(1024)(128)(4,1)} %bitcast.170), calls=%async_computation.8 | async-start | bytes 8388608
  406.3 6.5 %slice-start.5 = ((s8[8388608]{0:T(1024)(128)(4,1)}), s8[4194304]{0:T(1024)(128)(4,1)S(1)}, s32[]{:S(2)}) async-start(s8[8388608]{0:T(1024)(128)(4,1)} %bitcast.170), calls=%async_computation.9 | async-start | bytes 8388608
  420.7 76.5 %all-to-all-start.3 = ((bf16[2,1,2048,128]{3,0,1,2:T(2,128)(2,1)}), bf16[2,1,2048,128]{3,0,1,2:T(2,128)(2,1)S(1)}, u32[]{:S(2)}, u32[]{:S(2)}) async-start(bf16[2,1,2048,128]{3,0,1,2:T(2,128)(2,1)} %copy.74), calls=%async_computation.3 | async-start | bytes 2097152 | tf_op jit(solution)/shard_map/all_to_all | solution.py:157
  502.7 9.7 %slice-start.6 = ((s8[8388608]{0:T(1024)(128)(4,1)}), s8[4194304]{0:T(1024)(128)(4,1)S(1)}, s32[]{:S(2)}) async-start(s8[8388608]{0:T(1024)(128)(4,1)} %bitcast.174), calls=%async_computation.10 | async-start | bytes 8388608
  507.5 4.9 slice-start.7
  507.5 7.2 %copy-start.1 = (bf16[2,128,2304]{2,1,0:T(8,128)(2,1)S(1)}, bf16[2,128,2304]{2,1,0:T(8,128)(2,1)}, u32[]{:S(2)}) copy-start(bf16[2,128,2304]{2,1,0:T(8,128)(2,1)} %param.10) | copy-start | bytes 3538948
where the time goes:
time: 523 us; the launch traced here: 515 us
  matrix products  168 us (32%)
  other arithmetic  123 us (24%)
  local copies, waits for them, and re-layouts  95.4 us (18%)
  blocking collectives  89 us (17%)
  starting transfers between devices  21.1 us (4%)
  waiting for transfers between devices  15.4 us (3%)
    dynamic_update_slice x16, other arithmetic, dft_tables(): cosine, sine = lax.map(one_block, row_blocks)  90.7 us
    psum x1, blocking collectives, on_device(): lax.psum(lag_sums, ('det', 'frames')) / (frames_total * extent)  71.2 us
    dot_general x19, matrix products, turn(): jnp.einsum('syz,sfzn->fyn', weights, shifted, preferred_element_type=jnp....  64 us
    dot_general x8, matrix products, left_product(): jnp.einsum('km,fmr->fkr', table, values, preferred_element_type=jnp.float32)  41.8 us
    dot_general x19, matrix products, turn(): jnp.einsum('fyn,sfzn->syz', intensity_rows, shifted, preferred_element_ty...  34.2 us
    dot_general x8, matrix products, right_product(): jnp.einsum('frn,nl->frl', values, table, preferred_element_type=jnp.float32)  24.3 us
    unnamed x8, other arithmetic  23.7 us
    another operation x19, local copies, waits for them, and re-layouts, turn(): jnp.stack([lax.dynamic_slice_in_dim(padded, first_tap + tap_offset, exten...  20.6 us
  transfers between devices with their start and end apart: 5, of which 2 were waited for; matrix products, arithmetic and copies ran while one was open for 10% of the time, Pallas kernels for 0%

commit v1 on v0

v1 whole, which is shorter than its diff:
```python
import functools
import math

import jax
import jax.numpy as jnp
import ml_dtypes
import numpy as np
from jax import lax
from jax.experimental import pallas as pl
from jax.experimental.pallas import tpu as pltpu
from jax.sharding import PartitionSpec as P

MESH = pl.DeviceIdType.MESH
F32, BF16 = jnp.float32, jnp.bfloat16
N = 2048
HK = 28
TAPS = 2 * HK + 1
RADIX = 8
SUB = N // RADIX
BLK = 128
DET = N // BLK
ROOT_HALF = math.sqrt(0.5)


def as_bf16(values):
    return np.asarray(values, np.float32).astype(ml_dtypes.bfloat16)


@functools.cache
def tables():
    residue = np.arange(RADIX)[:, None, None]
    point = np.arange(SUB)[None, :, None]
    freq = np.arange(SUB)[None, None, :]
    angle = 2 * np.pi * (point * (RADIX * freq + residue) % N) / N
    cos, sin = np.cos(angle) / math.sqrt(N), np.sin(angle) / math.sqrt(N)
    forward = np.concatenate(
        [np.concatenate([cos, -sin], 2), np.concatenate([sin, cos], 2)], 1
    )
    inverse = np.swapaxes(forward, 1, 2)

    spread = np.zeros((1024, 1024))
    for r in range(RADIX):
        spread[RADIX * np.arange(BLK) + r, BLK * r + np.arange(BLK)] = 1

    lag = np.arange(64)
    ky = RADIX * np.arange(SUB)[None, :, None] + residue
    beta = 2 * np.pi * (ky * (lag[None, None, :] - HK) % N) / N
    used = (lag < TAPS)[None, None, :]
    cos, sin = np.cos(beta) * used, np.sin(beta) * used
    row_lags = np.concatenate(
        [np.concatenate([cos, -sin], 2), np.concatenate([sin, cos], 2)], 1
    )

    alpha = 2 * np.pi * (np.arange(BLK) + 0.5) / 256
    lane = np.arange(64)
    halo_u = np.where(lane < HK, lane, lane - HK + HK + BLK)
    halo_on = lane < 2 * HK
    u = np.concatenate([np.arange(BLK) + HK, halo_u, halo_u])
    on = np.concatenate([np.ones(BLK, bool), halo_on, halo_on])
    phase = alpha[:, None] * u[None, :]
    across = np.concatenate([np.cos(phase) * on, -np.sin(phase) * on], 0) / 16

    order = (RADIX * np.arange(16)[None, :] + np.arange(RADIX)[:, None]).reshape(-1)
    phase = alpha[:, None] * (order + HK)[None, :]
    across_own = np.concatenate([np.cos(phase), -np.sin(phase)], 0) / 16
    across_back = 2 * across_own.T

    pick = np.zeros((512, BLK))
    t = np.arange(HK)
    pick[BLK - HK + t, t] = 1
    pick[BLK + t, HK + t] = 1
    pick[256 + BLK - HK + t, 64 + t] = 1
    pick[384 + t, 64 + HK + t] = 1

    tap = np.arange(BLK)
    phase = alpha[:, None] * (tap - HK)[None, :]
    on = tap < TAPS
    kernel_x = np.concatenate([np.cos(phase) * on, np.sin(phase) * on], 1)
    tap = np.arange(BLK) % 64
    phase = alpha[:, None] * (tap - HK)[None, :]
    on = tap < TAPS
    lag_x = 2 * np.stack([np.cos(phase) * on, np.sin(phase) * on])
    return dict(
        forward=as_bf16(forward),
        inverse=as_bf16(inverse),
        spread=as_bf16(spread),
        row_lags=as_bf16(row_lags),
        across=as_bf16(across),
        across_own=as_bf16(across_own),
        across_back=as_bf16(across_back),
        pick=as_bf16(pick),
        eye=as_bf16(np.eye(BLK)),
        kernel_x=kernel_x.astype(np.float32),
        lag_x=lag_x.astype(np.float32),
    )


def dot(a, b):
    return jnp.dot(a, b, preferred_element_type=F32)


def dot_t(a, b):
    return lax.dot_general(a, b, (((1,), (1,)), ((), ())), preferred_element_type=F32)


def add(a, b):
    return (a[0] + b[0], a[1] + b[1])


def sub(a, b):
    return (a[0] - b[0], a[1] - b[1])


def dft4(z, sign):
    c0, c1 = add(z[0], z[2]), sub(z[0], z[2])
    d0, t = add(z[1], z[3]), sub(z[1], z[3])
    d1 = (-t[1], t[0]) if sign > 0 else (t[1], -t[0])
    return [add(c0, d0), add(c1, d1), sub(c0, d0), sub(c1, d1)]


def dft8(z, sign):
    a = [add(z[q], z[q + 4]) for q in range(4)]
    b = [sub(z[q], z[q + 4]) for q in range(4)]
    if sign > 0:
        b[1] = (ROOT_HALF * (b[1][0] - b[1][1]), ROOT_HALF * (b[1][1] + b[1][0]))
        b[2] = (-b[2][1], b[2][0])
        b[3] = (-ROOT_HALF * (b[3][0] + b[3][1]), ROOT_HALF * (b[3][0] - b[3][1]))
    else:
        b[1] = (ROOT_HALF * (b[1][0] + b[1][1]), ROOT_HALF * (b[1][1] - b[1][0]))
        b[2] = (b[2][1], -b[2][0])
        b[3] = (ROOT_HALF * (b[3][1] - b[3][0]), -ROOT_HALF * (b[3][1] + b[3][0]))
    even, odd = dft4(a, sign), dft4(b, sign)
    return [half for pair in zip(even, odd) for half in pair]


def split_residues(source, target):
    def body(step, carry):
        rows = pl.ds(pl.multiple_of(step * 16, 16), 16)
        for p in range(2):
            z = [
                tuple(source[2 * q + p, c, rows, :].astype(F32) for c in range(2))
                for q in range(RADIX)
            ]
            out = dft8(z, -1)
            for r in range(RADIX):
                for c in range(2):
                    first = c * SUB + p * BLK
                    target[r, rows, first : first + BLK] = out[r][c].astype(BF16)
        return carry

    lax.fori_loop(0, BLK // 16, body, 0)


def join_residues(source, store):
    def body(step, carry):
        rows = pl.ds(pl.multiple_of(step * 16, 16), 16)
        for p in range(2):
            z = [
                tuple(
                    source[r, rows, c * SUB + p * BLK : c * SUB + (p + 1) * BLK]
                    for c in range(2)
                )
                for r in range(RADIX)
            ]
            out = dft8(z, 1)
            for q in range(RADIX):
                for c in range(2):
                    store(2 * q + p, c, step, out[q][c].astype(BF16))
        return carry

    lax.fori_loop(0, BLK // 16, body, 0)


def loop(count, body):
    def step(index, carry):
        body(index)
        return carry

    lax.fori_loop(0, count, step, 0)


def kernel_body(
    frames,
    pos_ref, probe_ref, object_ref, cot_ref, taps_ref,
    across_ref, own_ref, back_ref, pick_ref, eye_ref, kx_ref, lagx_ref,
    fwd_hbm, inv_hbm, spread_hbm, lags_hbm,
    wave_ref, kgrad_ref,
    fwd, inv, spread, lags,
    cot_main, cot_halo, halo_out, wide, parts, sums, chat,
    half_out, half_in, back_out, back_in,
    ig_x, ig_nat, ig_perm, inten, inten_nat, tap_pad,
    kg_own, kg_frames, kg_det,
    table_sem, main_send, main_recv, halo_send, halo_recv,
    half_send, half_recv, back_send, back_recv, kgf_send, kgf_recv, kgd_send, kgd_recv,
):
    me = lax.axis_index("det")
    my_frame = lax.axis_index("frames")
    loads = [
        pltpu.make_async_copy(source, target, table_sem.at[index])
        for index, (source, target) in enumerate(
            ((inv_hbm, inv), (fwd_hbm, fwd), (lags_hbm, lags), (spread_hbm, spread))
        )
    ]
    for load in loads:
        load.start()

    def det_peer(offset):
        return lax.rem(me + offset, DET)

    def frame_peer(offset):
        return lax.rem(my_frame + offset, frames)

    barrier = pltpu.get_barrier_semaphore()
    loop(DET - 1, lambda o: pl.semaphore_signal(
        barrier, inc=1, device_id={"det": det_peer(o + 1)}, device_id_type=MESH))
    if frames > 1:
        loop(frames - 1, lambda o: pl.semaphore_signal(
            barrier, inc=1, device_id={"frames": frame_peer(o + 1)}, device_id_type=MESH))

    def exchange(source, target, send, recv):
        def copy(to, slot):
            return pltpu.make_async_remote_copy(
                src_ref=source(to),
                dst_ref=target.at[slot],
                send_sem=send.at[to],
                recv_sem=recv.at[slot],
                device_id={"det": to},
                device_id_type=MESH,
            )

        def start():
            loop(DET - 1, lambda o: copy(det_peer(o + 1), me).start())

        def wait_recv():
            loop(DET - 1, lambda o: copy(det_peer(o + 1), det_peer(o + 1)).wait_recv())

        def wait_send():
            loop(DET - 1, lambda o: copy(det_peer(o + 1), me).wait_send())

        return start, wait_recv, wait_send

    def lanes(block, width=BLK):
        return pl.ds(pl.multiple_of(block * width, width), width)

    main = exchange(lambda t: cot_ref.at[0, :, lanes(t)], cot_main, main_send, main_recv)
    halo = exchange(lambda t: halo_out.at[t], cot_halo, halo_send, halo_recv)
    half = exchange(lambda t: half_out.at[t], half_in, half_send, half_recv)
    back = exchange(lambda t: back_out.at[t], back_in, back_send, back_recv)

    def pack(block):
        before = lanes(lax.rem(block + DET - 1, DET))
        after = lanes(lax.rem(block + 1, DET))
        edges = jnp.concatenate(
            [
                cot_ref[0, rows, side]
                for rows in (pl.ds(0, 64), pl.ds(64, 64))
                for side in (before, after)
            ],
            axis=1,
        )
        halo_out[block] = dot(edges, pick_ref[...]).astype(BF16)

    loop(DET, pack)
    pl.semaphore_wait(barrier, DET - 1 + frames - 1)
    main[0]()
    halo[0]()

    position = pos_ref[0]
    distance = lax.broadcasted_iota(jnp.int32, (512, 256), 0) - lax.broadcasted_iota(
        jnp.int32, (512, 256), 1
    )
    shift = jnp.where(distance == position, 1.0, 0.0).astype(BF16)

    def exit_wave(q):
        wide_lanes = pl.ds(pl.multiple_of(q * 256, 256), 512)
        own = lanes(q, 256)
        w_re = dot(object_ref[0, :, wide_lanes], shift)
        w_im = dot(object_ref[1, :, wide_lanes], shift)
        p_re, p_im = probe_ref[0, :, own].astype(F32), probe_ref[1, :, own].astype(F32)
        re = (p_re * w_re - p_im * w_im).astype(BF16)
        im = (p_re * w_im + p_im * w_re).astype(BF16)
        for p in range(2):
            wide[2 * q + p, 0] = re[:, p * BLK : (p + 1) * BLK]
            wide[2 * q + p, 1] = im[:, p * BLK : (p + 1) * BLK]

    loop(RADIX, exit_wave)
    split_residues(wide, parts)
    loads[0].wait()

    def first_pass(r):
        out = dot_t(inv[r], parts[r]).astype(BF16).reshape(2, DET, 16, BLK)
        half_out[:, 0, lanes(r, 16), :] = out[0]
        half_out[:, 1, lanes(r, 16), :] = out[1]

    loop(RADIX, first_pass)
    half[0]()
    half_in[me] = half_out[me]

    tap_pad[...] = jnp.zeros_like(tap_pad)
    rounded = taps_ref[...].astype(BF16).astype(F32)
    tap_pad[0:TAPS, 0:TAPS] = rounded
    tap_pad[64 : 64 + TAPS, BLK : BLK + TAPS] = rounded
    tap_x = lax.dot_general(
        kx_ref[...], tap_pad[...], (((1,), (1,)), ((), ())),
        precision=lax.Precision.HIGHEST, preferred_element_type=F32,
    )
    tap_hi = tap_x.astype(BF16)
    tap_lo = (tap_x - tap_hi.astype(F32)).astype(BF16)

    cot_main[me] = cot_ref[0, :, lanes(me)]
    cot_halo[me] = halo_out[me]
    for load in loads[1:]:
        load.wait()
    main[1]()
    halo[1]()
    low = lax.broadcasted_iota(jnp.int32, (64, BLK), 1) < 64

    def cot_across(j):
        edge = cot_halo[j]
        zero = jnp.zeros_like(edge)
        spread_edge = jnp.concatenate(
            [jnp.where(low, edge, zero), jnp.where(low, zero, edge)], axis=0
        )
        both = jnp.concatenate([cot_main[j], spread_edge], axis=1)
        out = dot_t(across_ref[...], both).astype(BF16)
        wide[j, 0] = out[:BLK]
        wide[j, 1] = out[BLK:]

    loop(DET, cot_across)
    split_residues(wide, parts)

    def smooth(s):
        c = dot(parts[s], fwd[s])
        chat[s] = c
        k = dot_t(tap_hi, lags[s]) + dot_t(tap_lo, lags[s])
        c_re, c_im, k_re, k_im = c[:, :SUB], c[:, SUB:], k[:, :SUB], k[:, SUB:]
        g = jnp.concatenate(
            [c_re * k_re - c_im * k_im, c_re * k_im + c_im * k_re], axis=1
        )
        sums[s] = dot(g.astype(BF16), inv[s])

    loop(RADIX, smooth)

    def store_ig(block, c, step, value):
        rows = pl.ds(pl.multiple_of(c * BLK + step * 16, 16), 16)
        ig_x[rows, block * BLK : (block + 1) * BLK] = value

    join_residues(sums, store_ig)

    def ig_across(b):
        ig_nat[:, lanes(b, 256)] = dot(back_ref[...], ig_x[:, lanes(b, 256)]).astype(BF16)

    loop(RADIX, ig_across)
    for h in range(2):

        def to_residues(b, h=h):
            out = dot(ig_nat[:, h * 1024 : (h + 1) * 1024], spread[:, lanes(b, 256)])
            for p in range(2):
                ig_perm[2 * b + p, :, h * BLK : (h + 1) * BLK] = out[
                    :, p * BLK : (p + 1) * BLK
                ].astype(BF16)

        loop(4, to_residues)

    half[1]()
    split_residues(half_in, parts)

    def spectrum(r):
        x = dot(parts[r], fwd[r])
        re, im = x[:, :SUB], x[:, SUB:]
        intensity = (re * re + im * im).astype(BF16)
        for h in range(2):
            inten[h, :, lanes(r)] = intensity[:, h * BLK : (h + 1) * BLK]
        twice = 2.0 * ig_perm[r].astype(F32)
        grad = jnp.concatenate([(twice * re).astype(BF16), (twice * im).astype(BF16)], axis=1)
        sums[r] = dot(grad, inv[r])

    loop(RADIX, spectrum)

    def store_back(block, c, step, value):
        rows = pl.ds(pl.multiple_of(step * 16, 16), 16)
        back_out[block, c, rows, :] = value

    join_residues(sums, store_back)
    back[0]()
    back_in[me] = back_out[me]

    for h in range(2):

        def to_natural(b, h=h):
            out = dot_t(inten[h], spread[lanes(b, 256), :]).astype(BF16)
            inten_nat[:, pl.ds(pl.multiple_of(h * 1024 + b * 256, 256), 256)] = out

        loop(4, to_natural)

    def inten_across(b):
        out = dot(own_ref[...], inten_nat[:, lanes(b, 256)]).astype(BF16)
        for p in range(2):
            for c in range(2):
                wide[2 * b + p, c] = out[c * BLK : (c + 1) * BLK, p * BLK : (p + 1) * BLK]

    loop(RADIX, inten_across)
    split_residues(wide, parts)

    def lag_sums(s, total):
        x = dot(parts[s], fwd[s])
        c = chat[s]
        x_re, x_im, c_re, c_im = x[:, :SUB], x[:, SUB:], c[:, :SUB], c[:, SUB:]
        product = jnp.concatenate(
            [x_re * c_re + x_im * c_im, x_im * c_re - x_re * c_im], axis=1
        )
        return total + dot(product.astype(BF16), lags[s])

    by_lag = lax.fori_loop(0, RADIX, lag_sums, jnp.zeros((BLK, BLK), F32)).T
    kg = sum(
        lax.dot_general(
            by_lag[c * 64 : (c + 1) * 64], lagx_ref[c], (((1,), (0,)), ((), ())),
            precision=lax.Precision.HIGHEST, preferred_element_type=F32,
        )
        for c in range(2)
    ) * (1.0 / (frames * N))
    first = lax.broadcasted_iota(jnp.int32, (32, BLK), 1) < 64
    kg_own[0] = jnp.where(first, kg[:32], kg[32:])

    def frame_copy(to, slot):
        return pltpu.make_async_remote_copy(
            src_ref=kg_own.at[0],
            dst_ref=kg_frames.at[slot],
            send_sem=kgf_send.at[to],
            recv_sem=kgf_recv.at[slot],
            device_id={"frames": to},
            device_id_type=MESH,
        )

    if frames > 1:
        loop(frames - 1, lambda o: frame_copy(frame_peer(o + 1), my_frame).start())
    kg_frames[my_frame] = kg_own[0]
    if frames > 1:
        loop(frames - 1, lambda o: frame_copy(frame_peer(o + 1), frame_peer(o + 1)).wait_recv())
    kg_own[1] = sum(kg_frames[f] for f in range(frames))
    over_det = exchange(lambda t: kg_own.at[1], kg_det, kgd_send, kgd_recv)
    over_det[0]()
    kg_det[me] = kg_own[1]

    back[1]()

    def last_pass(r):
        turned = [
            dot_t(eye_ref[...], back_in[:, c, lanes(r, 16), :].reshape(SUB, BLK)).astype(BF16)
            for c in range(2)
        ]
        sums[r] = dot(jnp.concatenate(turned, axis=1), inv[r])

    loop(RADIX, last_pass)

    def store_wave(block, c, step, value):
        rows = pl.ds(pl.multiple_of(step * 16, 16), 16)
        wave_ref[c, 0, rows, block * BLK : (block + 1) * BLK] = value

    join_residues(sums, store_wave)

    over_det[1]()
    total = sum(kg_det[j] for j in range(DET))
    kgrad_ref[0:32, :] = total[:, 0:TAPS]
    kgrad_ref[32:TAPS, :] = pltpu.roll(total, 64, 1)[0 : TAPS - 32, 0:TAPS]

    for kind in (main, halo, half, back, over_det):
        kind[2]()
    if frames > 1:
        loop(frames - 1, lambda o: frame_copy(frame_peer(o + 1), my_frame).wait_send())


def on_device(frames, probe, object_field, positions, cotangent, kernel):
    t = tables()
    vmem = pl.BlockSpec(memory_space=pltpu.VMEM)
    hbm = pl.BlockSpec(memory_space=pl.ANY)
    small = [t[k] for k in ("across", "across_own", "across_back", "pick", "eye", "kernel_x", "lag_x")]
    large = [t[k] for k in ("forward", "inverse", "spread", "row_lags")]
    sem = pltpu.SemaphoreType.DMA
    scratch = [pltpu.VMEM(x.shape, BF16) for x in large] + [
        pltpu.VMEM((DET, BLK, BLK), BF16),
        pltpu.VMEM((DET, 64, BLK), BF16),
        pltpu.VMEM((DET, 64, BLK), BF16),
        pltpu.VMEM((DET, 2, BLK, BLK), BF16),
        pltpu.VMEM((RADIX, BLK, 2 * SUB), BF16),
        pltpu.VMEM((RADIX, BLK, 2 * SUB), F32),
        pltpu.VMEM((RADIX, BLK, 2 * SUB), F32),
        pltpu.VMEM((DET, 2, BLK, BLK), BF16),
        pltpu.VMEM((DET, 2, BLK, BLK), BF16),
        pltpu.VMEM((DET, 2, BLK, BLK), BF16),
        pltpu.VMEM((DET, 2, BLK, BLK), BF16),
        pltpu.VMEM((2 * BLK, N), BF16),
        pltpu.VMEM((BLK, N), BF16),
        pltpu.VMEM((RADIX, BLK, SUB), BF16),
        pltpu.VMEM((2, BLK, N // 2), BF16),
        pltpu.VMEM((BLK, N), BF16),
        pltpu.VMEM((BLK, 2 * BLK), F32),
        pltpu.VMEM((2, 32, BLK), F32),
        pltpu.VMEM((frames, 32, BLK), F32),
        pltpu.VMEM((DET, 32, BLK), F32),
        sem((4,)),
    ]
    scratch += [sem((DET,))] * 8 + [sem((frames,))] * 2 + [sem((DET,))] * 2
    return pl.pallas_call(
        functools.partial(kernel_body, frames),
        out_shape=(
            jax.ShapeDtypeStruct((2, 1, BLK, N), BF16),
            jax.ShapeDtypeStruct((TAPS, TAPS), F32),
        ),
        in_specs=[pl.BlockSpec(memory_space=pltpu.SMEM)] + [vmem] * 11 + [hbm] * 4,
        out_specs=(vmem, vmem),
        scratch_shapes=scratch,
        compiler_params=pltpu.CompilerParams(
            collective_id=0, has_side_effects=True, vmem_limit_bytes=56 * 1024 * 1024
        ),
        cost_estimate=pl.CostEstimate(flops=6_000_000_000, bytes_accessed=16_000_000, transcendentals=0),
    )(positions, probe, object_field, cotangent, kernel, *small, *large)


def solution(mesh):
    frames = mesh.shape["frames"]
    placed = (
        P(None, "det", None),
        P(None, "det", None),
        P("frames"),
        P("frames", "det", None),
        P(),
    )
    return jax.shard_map(
        functools.partial(on_device, frames),
        mesh=mesh,
        in_specs=placed,
        out_specs=(P(None, "frames", "det", None), P()),
        check_vma=False,
    )
```

time: 523 us -> 70.6 us (0.13); the launches traced: 515 us -> 70.4 us
  matrix products: 168 us -> 0 us
  other arithmetic: 123 us -> 0 us
  local copies, waits for them, and re-layouts: 95.4 us -> 3.68 us
  blocking collectives: 89 us -> 0 us
  Pallas kernels: 0 us -> 65.4 us
  starting transfers between devices: 21.1 us -> 0 us
  waiting for transfers between devices: 15.4 us -> 0 us
    dot_general x55 -> x0, matrix products: 168 us -> none  [the longest x19 64 us: turn(): jnp.einsum('syz,sfzn->fyn', weights, shifted, preferred_element_type=jnp....]
    dynamic_update_slice x16 -> x0, other arithmetic: 90.7 us -> none  [dft_tables(): cosine, sine = lax.map(one_block, row_blocks)]
    psum x1 -> x0, blocking collectives: 71.2 us -> none  [on_device(): lax.psum(lag_sums, ('det', 'frames')) / (frames_total * extent)]
    pallas_call x0 -> x1, Pallas kernels: none -> 65.4 us  [on_device(): pl.pallas_call(functools.partial(kernel_body, frames), out_shape=(jax.Sha...]
    another operation x21 -> x0, local copies, waits for them, and re-layouts: 24.6 us -> none  [the longest x19 20.6 us: turn(): jnp.stack([lax.dynamic_slice_in_dim(padded, first_tap + tap_offset, exten...]
    unnamed x8 -> x0, other arithmetic: 23.7 us -> none
    all_to_all x3 -> x0, starting transfers between devices: 19 us -> none  [the longest x1 9.29 us: on_device(): lax.all_to_all(half_transform, 'det', split_axis=3, concat_axis=2, tiled=...]
    all_to_all x1 -> x0, blocking collectives: 17.8 us -> none  [on_device(): lax.all_to_all(gradient.astype(jnp.bfloat16), 'det', split_axis=2, concat...]
  transfers between devices with their start and end apart: 5 -> 0, of which waited for: 2 -> 0; matrix products, arithmetic and copies ran while one was open for 10% -> 0% of each run, Pallas kernels for 0% -> 0%
where the time goes in v1:
time: 70.6 us; the launch traced here: 70.4 us
  Pallas kernels  65.4 us (93%)
  local copies, waits for them, and re-layouts  3.68 us (5%)
  between operations  1.29 us (2%)
    pallas_call x1, Pallas kernels, on_device(): pl.pallas_call(functools.partial(kernel_body, frames), out_shape=(jax.Sha...  65.4 us
    unnamed x2, local copies, waits for them, and re-layouts  3.68 us

profile of v1, /device:TPU:1, one launch (start us, length us, event | category | flops | bytes accessed | tf_op | source)
XLA Modules:
  0.0 70.4 jit_solution(9542741232075000478)
XLA Ops:
  1.3 65.4 %shard_map.167 = (bf16[2,1,128,2048]{3,2,1,0:T(8,128)(2,1)}, f32[57,57]{1,0:T(8,128)}) custom-call(s32[1]{0:T(128)S(6)} %copy.20.pos_ref, bf16[2,128,2048]{2,1,0:T(8,128)(2,1)} %probe_ref.1, bf16[2,128,2304]{2,1,0:T(8,128)(2,1)} %object_ref.1, bf16[1,128,2048]{2,1,0:T(8,128)(2,1)} %cot_ref.1, f32[57,57]{1,0:T(8,128)} %taps_ref.1, ...), custom_call_target="tpu_custom_call" | custom-call | flops 6000000000 | bytes 16000000 | tf_op jit(solution)/shard_map/pallas_call | solution.py:504
  66.7 2.3 %copy.21 = bf16[2,1,128,2048]{3,2,1,0:T(8,128)(2,1)} copy(bf16[2,1,128,2048]{3,2,1,0:T(8,128)(2,1)} %get-tuple-element.4) | data formatting | bytes 2097152
  69.0 1.4 %copy.22 = f32[57,57]{1,0:T(8,128)} copy(f32[57,57]{1,0:T(8,128)} %get-tuple-element.5) | data formatting | bytes 25992

commit v2 on v1

--- a/solution.py
+++ b/solution.py
@@ -19,6 +19,8 @@
 SUB = N // RADIX
 BLK = 128
 DET = N // BLK
+PARTS = 2
+PART = BLK // PARTS
 ROOT_HALF = math.sqrt(0.5)
 
 
@@ -133,9 +135,9 @@
     return [half for pair in zip(even, odd) for half in pair]
 
 
-def split_residues(source, target):
+def split_residues(source, target, start=0, count=BLK):
     def body(step, carry):
-        rows = pl.ds(pl.multiple_of(step * 16, 16), 16)
+        rows = pl.ds(pl.multiple_of(start + step * 16, 16), 16)
         for p in range(2):
             z = [
                 tuple(source[2 * q + p, c, rows, :].astype(F32) for c in range(2))
@@ -148,12 +150,12 @@
                     target[r, rows, first : first + BLK] = out[r][c].astype(BF16)
         return carry
 
-    lax.fori_loop(0, BLK // 16, body, 0)
-
-
-def join_residues(source, store):
+    lax.fori_loop(0, count // 16, body, 0)
+
+
+def join_residues(source, store, start=0, count=BLK):
     def body(step, carry):
-        rows = pl.ds(pl.multiple_of(step * 16, 16), 16)
+        rows = pl.ds(pl.multiple_of(start + step * 16, 16), 16)
         for p in range(2):
             z = [
                 tuple(
@@ -165,18 +167,19 @@
             out = dft8(z, 1)
             for q in range(RADIX):
                 for c in range(2):
-                    store(2 * q + p, c, step, out[q][c].astype(BF16))
+                    store(2 * q + p, c, start + step * 16, out[q][c].astype(BF16))
         return carry
 
-    lax.fori_loop(0, BLK // 16, body, 0)
-
-
-def loop(count, body):
+    lax.fori_loop(0, count // 16, body, 0)
+
+
+def loop(count, body, unroll=1):
     def step(index, carry):
-        body(index)
+        for part in range(unroll):
+            body(index * unroll + part)
         return carry
 
-    lax.fori_loop(0, count, step, 0)
+    lax.fori_loop(0, count // unroll, step, 0)
 
 
 def kernel_body(
@@ -217,13 +220,13 @@
         loop(frames - 1, lambda o: pl.semaphore_signal(
             barrier, inc=1, device_id={"frames": frame_peer(o + 1)}, device_id_type=MESH))
 
-    def exchange(source, target, send, recv):
+    def exchange(source, target, send, recv, part=0):
         def copy(to, slot):
             return pltpu.make_async_remote_copy(
                 src_ref=source(to),
-                dst_ref=target.at[slot],
-                send_sem=send.at[to],
-                recv_sem=recv.at[slot],
+                dst_ref=target(slot),
+                send_sem=send.at[part, to],
+                recv_sem=recv.at[part, slot],
                 device_id={"det": to},
                 device_id_type=MESH,
             )
@@ -242,10 +245,22 @@
     def lanes(block, width=BLK):
         return pl.ds(pl.multiple_of(block * width, width), width)
 
-    main = exchange(lambda t: cot_ref.at[0, :, lanes(t)], cot_main, main_send, main_recv)
-    halo = exchange(lambda t: halo_out.at[t], cot_halo, halo_send, halo_recv)
-    half = exchange(lambda t: half_out.at[t], half_in, half_send, half_recv)
-    back = exchange(lambda t: back_out.at[t], back_in, back_send, back_recv)
+    def by_parts(source, target, send, recv):
+        return [
+            exchange(
+                lambda t, k=k: source.at[t, :, pl.ds(k * PART, PART), :],
+                lambda t, k=k: target.at[t, :, pl.ds(k * PART, PART), :],
+                send, recv, k,
+            )
+            for k in range(PARTS)
+        ]
+
+    main = exchange(
+        lambda t: cot_ref.at[0, :, lanes(t)], lambda t: cot_main.at[t], main_send, main_recv
+    )
+    halo = exchange(lambda t: halo_out.at[t], lambda t: cot_halo.at[t], halo_send, halo_recv)
+    half = by_parts(half_out, half_in, half_send, half_recv)
+    back = by_parts(back_out, back_in, back_send, back_recv)
 
     def pack(block):
         before = lanes(lax.rem(block + DET - 1, DET))
@@ -260,7 +275,7 @@
         )
         halo_out[block] = dot(edges, pick_ref[...]).astype(BF16)
 
-    loop(DET, pack)
+    loop(DET, pack, RADIX)
     pl.semaphore_wait(barrier, DET - 1 + frames - 1)
     main[0]()
     halo[0]()
@@ -283,7 +298,7 @@
             wide[2 * q + p, 0] = re[:, p * BLK : (p + 1) * BLK]
             wide[2 * q + p, 1] = im[:, p * BLK : (p + 1) * BLK]
 
-    loop(RADIX, exit_wave)
+    loop(RADIX, exit_wave, RADIX)
     split_residues(wide, parts)
     loads[0].wait()
 
@@ -292,8 +307,10 @@
         half_out[:, 0, lanes(r, 16), :] = out[0]
         half_out[:, 1, lanes(r, 16), :] = out[1]
 
-    loop(RADIX, first_pass)
-    half[0]()
+    for k in range(PARTS):
+        for r in range(k * RADIX // PARTS, (k + 1) * RADIX // PARTS):
+            first_pass(r)
+        half[k][0]()
     half_in[me] = half_out[me]
 
     tap_pad[...] = jnp.zeros_like(tap_pad)
@@ -326,7 +343,7 @@
         wide[j, 0] = out[:BLK]
         wide[j, 1] = out[BLK:]
 
-    loop(DET, cot_across)
+    loop(DET, cot_across, RADIX)
     split_residues(wide, parts)
 
     def smooth(s):
@@ -339,10 +356,10 @@
         )
         sums[s] = dot(g.astype(BF16), inv[s])
 
-    loop(RADIX, smooth)
-
-    def store_ig(block, c, step, value):
-        rows = pl.ds(pl.multiple_of(c * BLK + step * 16, 16), 16)
+    loop(RADIX, smooth, RADIX)
+
+    def store_ig(block, c, row, value):
+        rows = pl.ds(pl.multiple_of(c * BLK + row, 16), 16)
         ig_x[rows, block * BLK : (block + 1) * BLK] = value
 
     join_residues(sums, store_ig)
@@ -350,7 +367,7 @@
     def ig_across(b):
         ig_nat[:, lanes(b, 256)] = dot(back_ref[...], ig_x[:, lanes(b, 256)]).astype(BF16)
 
-    loop(RADIX, ig_across)
+    loop(RADIX, ig_across, RADIX)
     for h in range(2):
 
         def to_residues(b, h=h):
@@ -360,29 +377,29 @@
                     :, p * BLK : (p + 1) * BLK
                 ].astype(BF16)
 
-        loop(4, to_residues)
-
-    half[1]()
-    split_residues(half_in, parts)
-
-    def spectrum(r):
-        x = dot(parts[r], fwd[r])
+        loop(4, to_residues, 4)
+
+    def spectrum(r, rows):
+        x = dot(parts[r, rows, :], fwd[r])
         re, im = x[:, :SUB], x[:, SUB:]
         intensity = (re * re + im * im).astype(BF16)
         for h in range(2):
-            inten[h, :, lanes(r)] = intensity[:, h * BLK : (h + 1) * BLK]
-        twice = 2.0 * ig_perm[r].astype(F32)
+            inten[h, rows, r * BLK : (r + 1) * BLK] = intensity[:, h * BLK : (h + 1) * BLK]
+        twice = 2.0 * ig_perm[r, rows, :].astype(F32)
         grad = jnp.concatenate([(twice * re).astype(BF16), (twice * im).astype(BF16)], axis=1)
-        sums[r] = dot(grad, inv[r])
-
-    loop(RADIX, spectrum)
-
-    def store_back(block, c, step, value):
-        rows = pl.ds(pl.multiple_of(step * 16, 16), 16)
+        sums[r, rows, :] = dot(grad, inv[r])
+
+    def store_back(block, c, row, value):
+        rows = pl.ds(pl.multiple_of(row, 16), 16)
         back_out[block, c, rows, :] = value
 
-    join_residues(sums, store_back)
-    back[0]()
+    for k in range(PARTS):
+        half[k][1]()
+        split_residues(half_in, parts, k * PART, PART)
+        for r in range(RADIX):
+            spectrum(r, slice(k * PART, (k + 1) * PART))
+        join_residues(sums, store_back, k * PART, PART)
+        back[k][0]()
     back_in[me] = back_out[me]
 
     for h in range(2):
@@ -391,7 +408,7 @@
             out = dot_t(inten[h], spread[lanes(b, 256), :]).astype(BF16)
             inten_nat[:, pl.ds(pl.multiple_of(h * 1024 + b * 256, 256), 256)] = out
 
-        loop(4, to_natural)
+        loop(4, to_natural, 4)
 
     def inten_across(b):
         out = dot(own_ref[...], inten_nat[:, lanes(b, 256)]).astype(BF16)
@@ -399,7 +416,7 @@
             for c in range(2):
                 wide[2 * b + p, c] = out[c * BLK : (c + 1) * BLK, p * BLK : (p + 1) * BLK]
 
-    loop(RADIX, inten_across)
+    loop(RADIX, inten_across, RADIX)
     split_residues(wide, parts)
 
     def lag_sums(s, total):
@@ -411,7 +428,10 @@
         )
         return total + dot(product.astype(BF16), lags[s])
 
-    by_lag = lax.fori_loop(0, RADIX, lag_sums, jnp.zeros((BLK, BLK), F32)).T
+    by_lag = jnp.zeros((BLK, BLK), F32)
+    for s in range(RADIX):
+        by_lag = lag_sums(s, by_lag)
+    by_lag = by_lag.T
     kg = sum(
         lax.dot_general(
             by_lag[c * 64 : (c + 1) * 64], lagx_ref[c], (((1,), (0,)), ((), ())),
@@ -438,11 +458,11 @@
     if frames > 1:
         loop(frames - 1, lambda o: frame_copy(frame_peer(o + 1), frame_peer(o + 1)).wait_recv())
     kg_own[1] = sum(kg_frames[f] for f in range(frames))
-    over_det = exchange(lambda t: kg_own.at[1], kg_det, kgd_send, kgd_recv)
+    over_det = exchange(
+        lambda t: kg_own.at[1], lambda t: kg_det.at[t], kgd_send, kgd_recv
+    )
     over_det[0]()
     kg_det[me] = kg_own[1]
-
-    back[1]()
 
     def last_pass(r):
         turned = [
@@ -451,10 +471,13 @@
         ]
         sums[r] = dot(jnp.concatenate(turned, axis=1), inv[r])
 
-    loop(RADIX, last_pass)
-
-    def store_wave(block, c, step, value):
-        rows = pl.ds(pl.multiple_of(step * 16, 16), 16)
+    for k in range(PARTS):
+        back[k][1]()
+        for r in range(k * RADIX // PARTS, (k + 1) * RADIX // PARTS):
+            last_pass(r)
+
+    def store_wave(block, c, row, value):
+        rows = pl.ds(pl.multiple_of(row, 16), 16)
         wave_ref[c, 0, rows, block * BLK : (block + 1) * BLK] = value
 
     join_residues(sums, store_wave)
@@ -464,10 +487,21 @@
     kgrad_ref[0:32, :] = total[:, 0:TAPS]
     kgrad_ref[32:TAPS, :] = pltpu.roll(total, 64, 1)[0 : TAPS - 32, 0:TAPS]
 
-    for kind in (main, halo, half, back, over_det):
+    for kind in (main, halo, *half, *back, over_det):
         kind[2]()
     if frames > 1:
         loop(frames - 1, lambda o: frame_copy(frame_peer(o + 1), my_frame).wait_send())
+
+
+def hand_over(wave_in, kgrad_in, wave_out, kgrad_out, sems):
+    copies = [
+        pltpu.make_async_copy(wave_in, wave_out, sems.at[0]),
+        pltpu.make_async_copy(kgrad_in, kgrad_out, sems.at[1]),
+    ]
+    for copy in copies:
+        copy.start()
+    for copy in copies:
+        copy.wait()
 
 
 def on_device(frames, probe, object_field, positions, cotangent, kernel):
@@ -477,6 +511,10 @@
     small = [t[k] for k in ("across", "across_own", "across_back", "pick", "eye", "kernel_x", "lag_x")]
     large = [t[k] for k in ("forward", "inverse", "spread", "row_lags")]
     sem = pltpu.SemaphoreType.DMA
+    shapes = (
+        jax.ShapeDtypeStruct((2, 1, BLK, N), BF16),
+        jax.ShapeDtypeStruct((TAPS, TAPS), F32),
+    )
     scratch = [pltpu.VMEM(x.shape, BF16) for x in large] + [
         pltpu.VMEM((DET, BLK, BLK), BF16),
         pltpu.VMEM((DET, 64, BLK), BF16),
@@ -500,13 +538,11 @@
         pltpu.VMEM((DET, 32, BLK), F32),
         sem((4,)),
     ]
-    scratch += [sem((DET,))] * 8 + [sem((frames,))] * 2 + [sem((DET,))] * 2
-    return pl.pallas_call(
+    scratch += [sem((1, DET))] * 4 + [sem((PARTS, DET))] * 4
+    scratch += [sem((frames,))] * 2 + [sem((1, DET))] * 2
+    results = pl.pallas_call(
         functools.partial(kernel_body, frames),
-        out_shape=(
-            jax.ShapeDtypeStruct((2, 1, BLK, N), BF16),
-            jax.ShapeDtypeStruct((TAPS, TAPS), F32),
-        ),
+        out_shape=shapes,
         in_specs=[pl.BlockSpec(memory_space=pltpu.SMEM)] + [vmem] * 11 + [hbm] * 4,
         out_specs=(vmem, vmem),
         scratch_shapes=scratch,
@@ -515,6 +551,13 @@
         ),
         cost_estimate=pl.CostEstimate(flops=6_000_000_000, bytes_accessed=16_000_000, transcendentals=0),
     )(positions, probe, object_field, cotangent, kernel, *small, *large)
+    return pl.pallas_call(
+        hand_over,
+        out_shape=shapes,
+        in_specs=[vmem] * 2,
+        out_specs=(hbm, hbm),
+        scratch_shapes=[sem((2,))],
+    )(*results)
 
 
 def solution(mesh):

time: 70.6 us -> 61.2 us (0.87)
  Pallas kernels: 65.4 us -> 59.7 us
  local copies, waits for them, and re-layouts: 3.68 us -> 0 us
    pallas_call x1 -> x2, Pallas kernels: 65.4 us -> 59.7 us  [the longest x1 57.5 us: on_device(): pl.pallas_call(functools.partial(kernel_body, frames), out_shape=shapes,...]
    unnamed x2 -> x0, local copies, waits for them, and re-layouts: 3.68 us -> none
where the time goes in v2:
time: 61.2 us; the launch traced here: 61 us
  Pallas kernels  59.7 us (98%)
  between operations  1.28 us (2%)
    pallas_call x1, Pallas kernels, on_device(): pl.pallas_call(functools.partial(kernel_body, frames), out_shape=shapes,...  57.5 us
    pallas_call x1, Pallas kernels, on_device(): pl.pallas_call(hand_over, out_shape=shapes, in_specs=[vmem] * 2, out_spec...  2.22 us

profile of v2, /device:TPU:1, one launch (start us, length us, event | category | flops | bytes accessed | tf_op | source)
XLA Modules:
  0.0 61.0 jit_solution(7873150457442530264)
XLA Ops:
  1.3 57.5 %shard_map.167 = (bf16[2,1,128,2048]{3,2,1,0:T(8,128)(2,1)}, f32[57,57]{1,0:T(8,128)}) custom-call(s32[1]{0:T(128)S(6)} %copy.18.pos_ref, bf16[2,128,2048]{2,1,0:T(8,128)(2,1)} %probe_ref.1, bf16[2,128,2304]{2,1,0:T(8,128)(2,1)} %object_ref.1, bf16[1,128,2048]{2,1,0:T(8,128)(2,1)} %cot_ref.1, f32[57,57]{1,0:T(8,128)} %taps_ref.1, ...), custom_call_target="tpu_custom_call" | custom-call | flops 6000000000 | bytes 16000000 | tf_op jit(solution)/shard_map/pallas_call | solution.py:543
  58.8 2.2 %shard_map.168 = (bf16[2,1,128,2048]{3,2,1,0:T(8,128)(2,1)}, f32[57,57]{1,0:T(8,128)}) custom-call(bf16[2,1,128,2048]{3,2,1,0:T(8,128)(2,1)} %get-tuple-element.4.wave_in, f32[57,57]{1,0:T(8,128)} %get-tuple-element.5.kgrad_in), custom_call_target="tpu_custom_call" | custom-call | tf_op jit(solution)/shard_map/pallas_call | solution.py:554

commit v3 on v2

--- a/solution.py
+++ b/solution.py
@@ -26,6 +26,12 @@
 
 def as_bf16(values):
     return np.asarray(values, np.float32).astype(ml_dtypes.bfloat16)
+
+
+LOADED = (
+    "cotangent", "pick", "object", "probe", "inverse", "taps", "kernel_x", "across",
+    "forward", "row_lags", "across_back", "spread", "across_own", "lag_x", "eye",
+)
 
 
 @functools.cache
@@ -184,28 +190,26 @@
 
 def kernel_body(
     frames,
-    pos_ref, probe_ref, object_ref, cot_ref, taps_ref,
-    across_ref, own_ref, back_ref, pick_ref, eye_ref, kx_ref, lagx_ref,
-    fwd_hbm, inv_hbm, spread_hbm, lags_hbm,
-    wave_ref, kgrad_ref,
-    fwd, inv, spread, lags,
-    cot_main, cot_halo, halo_out, wide, parts, sums, chat,
-    half_out, half_in, back_out, back_in,
-    ig_x, ig_nat, ig_perm, inten, inten_nat, tap_pad,
-    kg_own, kg_frames, kg_det,
-    table_sem, main_send, main_recv, halo_send, halo_recv,
-    half_send, half_recv, back_send, back_recv, kgf_send, kgf_recv, kgd_send, kgd_recv,
+    pos_ref, *refs,
 ):
     me = lax.axis_index("det")
     my_frame = lax.axis_index("frames")
-    loads = [
-        pltpu.make_async_copy(source, target, table_sem.at[index])
-        for index, (source, target) in enumerate(
-            ((inv_hbm, inv), (fwd_hbm, fwd), (lags_hbm, lags), (spread_hbm, spread))
-        )
-    ]
-    for load in loads:
-        load.start()
+    count = len(LOADED)
+    sources, (wave_ref, kgrad_ref), held = refs[:count], refs[count : count + 2], refs[count + 2 :]
+    held, rest = held[:count], held[count:]
+    (
+        cot_ref, pick_ref, object_ref, probe_ref, inv, taps_ref, kx_ref, across_ref,
+        fwd, lags, back_ref, spread, own_ref, lagx_ref, eye_ref,
+    ) = held
+    (
+        cot_main, cot_halo, halo_out, wide, parts, sums, chat,
+        spec, half_out, half_in, back_out, back_in,
+        ig_x, ig_nat, ig_perm, inten, inten_nat, tap_pad,
+        kg_own, kg_frames, kg_sum, kg_det,
+        load_sem, main_send, main_recv, halo_send, halo_recv,
+        half_send, half_recv, back_send, back_recv,
+        kgf_send, kgf_recv, kgd_send, kgd_recv,
+    ) = rest
 
     def det_peer(offset):
         return lax.rem(me + offset, DET)
@@ -219,6 +223,17 @@
     if frames > 1:
         loop(frames - 1, lambda o: pl.semaphore_signal(
             barrier, inc=1, device_id={"frames": frame_peer(o + 1)}, device_id_type=MESH))
+    loads = {
+        name: pltpu.make_async_copy(source, target, load_sem.at[index])
+        for index, (name, source, target) in enumerate(zip(LOADED, sources, held))
+    }
+    for load in loads.values():
+        load.start()
+
+    def ready(*names):
+        for name in names:
+            loads[name].wait()
+
 
     def exchange(source, target, send, recv, part=0):
         def copy(to, slot):
@@ -275,9 +290,11 @@
         )
         halo_out[block] = dot(edges, pick_ref[...]).astype(BF16)
 
-    loop(DET, pack, RADIX)
+    ready("cotangent")
     pl.semaphore_wait(barrier, DET - 1 + frames - 1)
     main[0]()
+    ready("pick")
+    loop(DET, pack, RADIX)
     halo[0]()
 
     position = pos_ref[0]
@@ -298,9 +315,10 @@
             wide[2 * q + p, 0] = re[:, p * BLK : (p + 1) * BLK]
             wide[2 * q + p, 1] = im[:, p * BLK : (p + 1) * BLK]
 
+    ready("object", "probe")
     loop(RADIX, exit_wave, RADIX)
     split_residues(wide, parts)
-    loads[0].wait()
+    ready("inverse")
 
     def first_pass(r):
         out = dot_t(inv[r], parts[r]).astype(BF16).reshape(2, DET, 16, BLK)
@@ -310,9 +328,13 @@
     for k in range(PARTS):
         for r in range(k * RADIX // PARTS, (k + 1) * RADIX // PARTS):
             first_pass(r)
+        if k == 0:
+            main[2]()
+            halo[2]()
         half[k][0]()
     half_in[me] = half_out[me]
 
+    ready("taps", "kernel_x")
     tap_pad[...] = jnp.zeros_like(tap_pad)
     rounded = taps_ref[...].astype(BF16).astype(F32)
     tap_pad[0:TAPS, 0:TAPS] = rounded
@@ -326,8 +348,7 @@
 
     cot_main[me] = cot_ref[0, :, lanes(me)]
     cot_halo[me] = halo_out[me]
-    for load in loads[1:]:
-        load.wait()
+    ready("across", "forward", "row_lags", "across_back", "spread", "across_own", "lag_x", "eye")
     main[1]()
     halo[1]()
     low = lax.broadcasted_iota(jnp.int32, (64, BLK), 1) < 64
@@ -385,6 +406,11 @@
         intensity = (re * re + im * im).astype(BF16)
         for h in range(2):
             inten[h, rows, r * BLK : (r + 1) * BLK] = intensity[:, h * BLK : (h + 1) * BLK]
+        spec[r, rows, :] = x
+
+    def gradient(r, rows):
+        x = spec[r, rows, :]
+        re, im = x[:, :SUB], x[:, SUB:]
         twice = 2.0 * ig_perm[r, rows, :].astype(F32)
         grad = jnp.concatenate([(twice * re).astype(BF16), (twice * im).astype(BF16)], axis=1)
         sums[r, rows, :] = dot(grad, inv[r])
@@ -392,15 +418,20 @@
     def store_back(block, c, row, value):
         rows = pl.ds(pl.multiple_of(row, 16), 16)
         back_out[block, c, rows, :] = value
+
+    def send_back(k):
+        for r in range(RADIX):
+            gradient(r, slice(k * PART, (k + 1) * PART))
+        join_residues(sums, store_back, k * PART, PART)
+        back[k][0]()
 
     for k in range(PARTS):
         half[k][1]()
         split_residues(half_in, parts, k * PART, PART)
         for r in range(RADIX):
             spectrum(r, slice(k * PART, (k + 1) * PART))
-        join_residues(sums, store_back, k * PART, PART)
-        back[k][0]()
-    back_in[me] = back_out[me]
+        if k < PARTS - 1:
+            send_back(k)
 
     for h in range(2):
 
@@ -442,27 +473,38 @@
     first = lax.broadcasted_iota(jnp.int32, (32, BLK), 1) < 64
     kg_own[0] = jnp.where(first, kg[:32], kg[32:])
 
-    def frame_copy(to, slot):
-        return pltpu.make_async_remote_copy(
-            src_ref=kg_own.at[0],
-            dst_ref=kg_frames.at[slot],
-            send_sem=kgf_send.at[to],
-            recv_sem=kgf_recv.at[slot],
-            device_id={"frames": to},
-            device_id_type=MESH,
-        )
-
-    if frames > 1:
-        loop(frames - 1, lambda o: frame_copy(frame_peer(o + 1), my_frame).start())
+    def over_frames(source, target, send, recv):
+        def copy(to, slot):
+            return pltpu.make_async_remote_copy(
+                src_ref=source(to),
+                dst_ref=target.at[slot],
+                send_sem=send.at[to],
+                recv_sem=recv.at[slot],
+                device_id={"frames": to},
+                device_id_type=MESH,
+            )
+
+        def start():
+            loop(frames - 1, lambda o: copy(frame_peer(o + 1), my_frame).start())
+
+        def wait_recv():
+            loop(frames - 1, lambda o: copy(frame_peer(o + 1), frame_peer(o + 1)).wait_recv())
+
+        def wait_send():
+            loop(frames - 1, lambda o: copy(frame_peer(o + 1), my_frame).wait_send())
+
+        return start, wait_recv, wait_send
+
+    across_frames = over_frames(lambda f: kg_own.at[0], kg_frames, kgf_send, kgf_recv)
+    over_det = exchange(lambda t: kg_sum.at[0], lambda t: kg_det.at[t], kgd_send, kgd_recv)
+    across_frames[0]()
     kg_frames[my_frame] = kg_own[0]
-    if frames > 1:
-        loop(frames - 1, lambda o: frame_copy(frame_peer(o + 1), frame_peer(o + 1)).wait_recv())
-    kg_own[1] = sum(kg_frames[f] for f in range(frames))
-    over_det = exchange(
-        lambda t: kg_own.at[1], lambda t: kg_det.at[t], kgd_send, kgd_recv
-    )
+    send_back(PARTS - 1)
+    back_in[me] = back_out[me]
+    across_frames[1]()
+    kg_sum[0] = sum(kg_frames[f] for f in range(frames))
     over_det[0]()
-    kg_det[me] = kg_own[1]
+    kg_det[me] = kg_sum[0]
 
     def last_pass(r):
         turned = [
@@ -487,10 +529,8 @@
     kgrad_ref[0:32, :] = total[:, 0:TAPS]
     kgrad_ref[32:TAPS, :] = pltpu.roll(total, 64, 1)[0 : TAPS - 32, 0:TAPS]
 
-    for kind in (main, halo, *half, *back, over_det):
+    for kind in (*half, *back, across_frames, over_det):
         kind[2]()
-    if frames > 1:
-        loop(frames - 1, lambda o: frame_copy(frame_peer(o + 1), my_frame).wait_send())
 
 
 def hand_over(wave_in, kgrad_in, wave_out, kgrad_out, sems):
@@ -505,22 +545,24 @@
 
 
 def on_device(frames, probe, object_field, positions, cotangent, kernel):
-    t = tables()
     vmem = pl.BlockSpec(memory_space=pltpu.VMEM)
     hbm = pl.BlockSpec(memory_space=pl.ANY)
-    small = [t[k] for k in ("across", "across_own", "across_back", "pick", "eye", "kernel_x", "lag_x")]
-    large = [t[k] for k in ("forward", "inverse", "spread", "row_lags")]
+    arrays = dict(
+        tables(), cotangent=cotangent, object=object_field, probe=probe, taps=kernel
+    )
+    arrays = [arrays[name] for name in LOADED]
     sem = pltpu.SemaphoreType.DMA
     shapes = (
         jax.ShapeDtypeStruct((2, 1, BLK, N), BF16),
         jax.ShapeDtypeStruct((TAPS, TAPS), F32),
     )
-    scratch = [pltpu.VMEM(x.shape, BF16) for x in large] + [
+    scratch = [pltpu.VMEM(x.shape, x.dtype) for x in arrays] + [
         pltpu.VMEM((DET, BLK, BLK), BF16),
         pltpu.VMEM((DET, 64, BLK), BF16),
         pltpu.VMEM((DET, 64, BLK), BF16),
         pltpu.VMEM((DET, 2, BLK, BLK), BF16),
         pltpu.VMEM((RADIX, BLK, 2 * SUB), BF16),
+        pltpu.VMEM((RADIX, BLK, 2 * SUB), F32),
         pltpu.VMEM((RADIX, BLK, 2 * SUB), F32),
         pltpu.VMEM((RADIX, BLK, 2 * SUB), F32),
         pltpu.VMEM((DET, 2, BLK, BLK), BF16),
@@ -533,24 +575,25 @@
         pltpu.VMEM((2, BLK, N // 2), BF16),
         pltpu.VMEM((BLK, N), BF16),
         pltpu.VMEM((BLK, 2 * BLK), F32),
-        pltpu.VMEM((2, 32, BLK), F32),
+        pltpu.VMEM((1, 32, BLK), F32),
         pltpu.VMEM((frames, 32, BLK), F32),
+        pltpu.VMEM((1, 32, BLK), F32),
         pltpu.VMEM((DET, 32, BLK), F32),
-        sem((4,)),
+        sem((len(arrays),)),
     ]
     scratch += [sem((1, DET))] * 4 + [sem((PARTS, DET))] * 4
     scratch += [sem((frames,))] * 2 + [sem((1, DET))] * 2
     results = pl.pallas_call(
         functools.partial(kernel_body, frames),
         out_shape=shapes,
-        in_specs=[pl.BlockSpec(memory_space=pltpu.SMEM)] + [vmem] * 11 + [hbm] * 4,
+        in_specs=[pl.BlockSpec(memory_space=pltpu.SMEM)] + [hbm] * len(arrays),
         out_specs=(vmem, vmem),
         scratch_shapes=scratch,
         compiler_params=pltpu.CompilerParams(
-            collective_id=0, has_side_effects=True, vmem_limit_bytes=56 * 1024 * 1024
+            collective_id=0, has_side_effects=True, vmem_limit_bytes=60 * 1024 * 1024
         ),
         cost_estimate=pl.CostEstimate(flops=6_000_000_000, bytes_accessed=16_000_000, transcendentals=0),
-    )(positions, probe, object_field, cotangent, kernel, *small, *large)
+    )(positions, *arrays)
     return pl.pallas_call(
         hand_over,
         out_shape=shapes,

time: 61.2 us -> 56.4 us (0.922)
  Pallas kernels: 59.7 us -> 55 us
    pallas_call x1, Pallas kernels: 57.5 us -> 52.7 us  [on_device(): pl.pallas_call(functools.partial(kernel_body, frames), out_shape=shapes,...]
where the time goes in v3:
time: 56.4 us; the launch traced here: 56.2 us
  Pallas kernels  55 us (98%)
  between operations  1.28 us (2%)
    pallas_call x1, Pallas kernels, on_device(): pl.pallas_call(functools.partial(kernel_body, frames), out_shape=shapes,...  52.7 us
    pallas_call x1, Pallas kernels, on_device(): pl.pallas_call(hand_over, out_shape=shapes, in_specs=[vmem] * 2, out_spec...  2.22 us

profile of v3, /device:TPU:1, one launch (start us, length us, event | category | flops | bytes accessed | tf_op | source)
XLA Modules:
  0.0 56.2 jit_solution(14210276357609977481)
XLA Ops:
  1.3 52.7 %shard_map.167 = (bf16[2,1,128,2048]{3,2,1,0:T(8,128)(2,1)}, f32[57,57]{1,0:T(8,128)}) custom-call(s32[1]{0:T(128)S(6)} %copy.18.pos_ref, bf16[1,128,2048]{2,1,0:T(8,128)(2,1)} %refs_0_.1, bf16[512,128]{1,0:T(8,128)(2,1)} %constant.22.clone.refs_1_, bf16[2,128,2304]{2,1,0:T(8,128)(2,1)} %refs_2_.1, bf16[2,128,2048]{2,1,0:T(8,128)(2,1)} %refs_3_.1, ...), custom_call_target="tpu_custom_call" | custom-call | flops 6000000000 | bytes 16000000 | tf_op jit(solution)/shard_map/pallas_call | solution.py:586
  54.0 2.2 %shard_map.168 = (bf16[2,1,128,2048]{3,2,1,0:T(8,128)(2,1)}, f32[57,57]{1,0:T(8,128)}) custom-call(bf16[2,1,128,2048]{3,2,1,0:T(8,128)(2,1)} %get-tuple-element.4.wave_in, f32[57,57]{1,0:T(8,128)} %get-tuple-element.5.kgrad_in), custom_call_target="tpu_custom_call" | custom-call | tf_op jit(solution)/shard_map/pallas_call | solution.py:597

commit v4 on v3

--- a/solution.py
+++ b/solution.py
@@ -19,8 +19,8 @@
 SUB = N // RADIX
 BLK = 128
 DET = N // BLK
-PARTS = 2
-PART = BLK // PARTS
+SPLIT = ((0, 64), (64, 64))
+PARTS = len(SPLIT)
 ROOT_HALF = math.sqrt(0.5)
 
 
@@ -217,18 +217,20 @@
     def frame_peer(offset):
         return lax.rem(my_frame + offset, frames)
 
+    loads = {
+        name: pltpu.make_async_copy(source, target, load_sem.at[index])
+        for index, (name, source, target) in enumerate(zip(LOADED, sources, held))
+    }
+    loads[LOADED[0]].start()
+
     barrier = pltpu.get_barrier_semaphore()
     loop(DET - 1, lambda o: pl.semaphore_signal(
         barrier, inc=1, device_id={"det": det_peer(o + 1)}, device_id_type=MESH))
     if frames > 1:
         loop(frames - 1, lambda o: pl.semaphore_signal(
             barrier, inc=1, device_id={"frames": frame_peer(o + 1)}, device_id_type=MESH))
-    loads = {
-        name: pltpu.make_async_copy(source, target, load_sem.at[index])
-        for index, (name, source, target) in enumerate(zip(LOADED, sources, held))
-    }
-    for load in loads.values():
-        load.start()
+    for name in LOADED[1:]:
+        loads[name].start()
 
     def ready(*names):
         for name in names:
@@ -263,11 +265,11 @@
     def by_parts(source, target, send, recv):
         return [
             exchange(
-                lambda t, k=k: source.at[t, :, pl.ds(k * PART, PART), :],
-                lambda t, k=k: target.at[t, :, pl.ds(k * PART, PART), :],
+                lambda t, cut=pl.ds(*cut): source.at[t, :, cut, :],
+                lambda t, cut=pl.ds(*cut): target.at[t, :, cut, :],
                 send, recv, k,
             )
-            for k in range(PARTS)
+            for k, cut in enumerate(SPLIT)
         ]
 
     main = exchange(
@@ -326,7 +328,7 @@
         half_out[:, 1, lanes(r, 16), :] = out[1]
 
     for k in range(PARTS):
-        for r in range(k * RADIX // PARTS, (k + 1) * RADIX // PARTS):
+        for r in range(SPLIT[k][0] // 16, sum(SPLIT[k]) // 16):
             first_pass(r)
         if k == 0:
             main[2]()
@@ -421,15 +423,15 @@
 
     def send_back(k):
         for r in range(RADIX):
-            gradient(r, slice(k * PART, (k + 1) * PART))
-        join_residues(sums, store_back, k * PART, PART)
+            gradient(r, slice(SPLIT[k][0], sum(SPLIT[k])))
+        join_residues(sums, store_back, *SPLIT[k])
         back[k][0]()
 
     for k in range(PARTS):
         half[k][1]()
-        split_residues(half_in, parts, k * PART, PART)
+        split_residues(half_in, parts, *SPLIT[k])
         for r in range(RADIX):
-            spectrum(r, slice(k * PART, (k + 1) * PART))
+            spectrum(r, slice(SPLIT[k][0], sum(SPLIT[k])))
         if k < PARTS - 1:
             send_back(k)
 
@@ -515,7 +517,7 @@
 
     for k in range(PARTS):
         back[k][1]()
-        for r in range(k * RADIX // PARTS, (k + 1) * RADIX // PARTS):
+        for r in range(SPLIT[k][0] // 16, sum(SPLIT[k]) // 16):
             last_pass(r)
 
     def store_wave(block, c, row, value):
@@ -533,15 +535,21 @@
         kind[2]()
 
 
-def hand_over(wave_in, kgrad_in, wave_out, kgrad_out, sems):
-    copies = [
-        pltpu.make_async_copy(wave_in, wave_out, sems.at[0]),
-        pltpu.make_async_copy(kgrad_in, kgrad_out, sems.at[1]),
-    ]
-    for copy in copies:
-        copy.start()
-    for copy in copies:
-        copy.wait()
+def hand_over(wave_in, kgrad_in, wave_out, kgrad_out, wave, kgrad, sems):
+    pairs = [(kgrad_in, kgrad, kgrad_out)]
+    for c in range(2):
+        for first in range(0, BLK, 64):
+            at = (c, 0, pl.ds(first, 64))
+            pairs.append((wave_in.at[at], wave.at[at], wave_out.at[at]))
+    loads = [pltpu.make_async_copy(a, b, sems.at[0, i]) for i, (a, b, _) in enumerate(pairs)]
+    stores = [pltpu.make_async_copy(b, c, sems.at[1, i]) for i, (_, b, c) in enumerate(pairs)]
+    for load in loads:
+        load.start()
+    for load, store in zip(loads, stores):
+        load.wait()
+        store.start()
+    for store in stores:
+        store.wait()
 
 
 def on_device(frames, probe, object_field, positions, cotangent, kernel):
@@ -597,9 +605,14 @@
     return pl.pallas_call(
         hand_over,
         out_shape=shapes,
-        in_specs=[vmem] * 2,
+        in_specs=[hbm] * 2,
         out_specs=(hbm, hbm),
-        scratch_shapes=[sem((2,))],
+        scratch_shapes=[
+            pltpu.VMEM(shapes[0].shape, BF16),
+            pltpu.VMEM(shapes[1].shape, F32),
+            sem((2, 5)),
+        ],
+        compiler_params=pltpu.CompilerParams(vmem_limit_bytes=60 * 1024 * 1024),
     )(*results)
 
 

time: 56.4 us -> 56.2 us (level)
  no operation moved by 1% of the time
where the time goes in v4:
time: 56.2 us; the launch traced here: 56.1 us
  Pallas kernels  54.8 us (98%)
  between operations  1.28 us (2%)
    pallas_call x1, Pallas kernels, on_device(): pl.pallas_call(functools.partial(kernel_body, frames), out_shape=shapes,...  52.8 us
    pallas_call x1, Pallas kernels, on_device(): pl.pallas_call(hand_over, out_shape=shapes, in_specs=[hbm] * 2, out_specs...  2.02 us

profile of v4, /device:TPU:1, one launch (start us, length us, event | category | flops | bytes accessed | tf_op | source)
XLA Modules:
  0.0 56.1 jit_solution(7221166452464417788)
XLA Ops:
  1.3 52.8 %shard_map.167 = (bf16[2,1,128,2048]{3,2,1,0:T(8,128)(2,1)}, f32[57,57]{1,0:T(8,128)}) custom-call(s32[1]{0:T(128)S(6)} %copy.18.pos_ref, bf16[1,128,2048]{2,1,0:T(8,128)(2,1)} %refs_0_.1, bf16[512,128]{1,0:T(8,128)(2,1)} %constant.22.clone.refs_1_, bf16[2,128,2304]{2,1,0:T(8,128)(2,1)} %refs_2_.1, bf16[2,128,2048]{2,1,0:T(8,128)(2,1)} %refs_3_.1, ...), custom_call_target="tpu_custom_call" | custom-call | flops 6000000000 | bytes 16000000 | tf_op jit(solution)/shard_map/pallas_call | solution.py:594
  54.0 2.0 %shard_map.168 = (bf16[2,1,128,2048]{3,2,1,0:T(8,128)(2,1)}, f32[57,57]{1,0:T(8,128)}) custom-call(bf16[2,1,128,2048]{3,2,1,0:T(8,128)(2,1)} %get-tuple-element.4.wave_in, f32[57,57]{1,0:T(8,128)} %get-tuple-element.5.kgrad_in), custom_call_target="tpu_custom_call" | custom-call | tf_op jit(solution)/shard_map/pallas_call | solution.py:605

commit v5 on v4

--- a/solution.py
+++ b/solution.py
@@ -503,10 +503,6 @@
     kg_frames[my_frame] = kg_own[0]
     send_back(PARTS - 1)
     back_in[me] = back_out[me]
-    across_frames[1]()
-    kg_sum[0] = sum(kg_frames[f] for f in range(frames))
-    over_det[0]()
-    kg_det[me] = kg_sum[0]
 
     def last_pass(r):
         turned = [
@@ -519,6 +515,11 @@
         back[k][1]()
         for r in range(SPLIT[k][0] // 16, sum(SPLIT[k]) // 16):
             last_pass(r)
+        if k == PARTS - 2:
+            across_frames[1]()
+            kg_sum[0] = sum(kg_frames[f] for f in range(frames))
+            over_det[0]()
+            kg_det[me] = kg_sum[0]
 
     def store_wave(block, c, row, value):
         rows = pl.ds(pl.multiple_of(row, 16), 16)

time: 56.2 us -> 56.2 us (level)
  no operation moved by 1% of the time
where the time goes in v5:
time: 56.2 us; the launch traced here: 56.1 us
  Pallas kernels  54.8 us (98%)
  between operations  1.28 us (2%)
    pallas_call x1, Pallas kernels, on_device(): pl.pallas_call(functools.partial(kernel_body, frames), out_shape=shapes,...  52.8 us
    pallas_call x1, Pallas kernels, on_device(): pl.pallas_call(hand_over, out_shape=shapes, in_specs=[hbm] * 2, out_specs...  2.02 us

profile of v5, /device:TPU:1, one launch (start us, length us, event | category | flops | bytes accessed | tf_op | source)
XLA Modules:
  0.0 56.1 jit_solution(3603603925479951569)
XLA Ops:
  1.3 52.8 %shard_map.167 = (bf16[2,1,128,2048]{3,2,1,0:T(8,128)(2,1)}, f32[57,57]{1,0:T(8,128)}) custom-call(s32[1]{0:T(128)S(6)} %copy.18.pos_ref, bf16[1,128,2048]{2,1,0:T(8,128)(2,1)} %refs_0_.1, bf16[512,128]{1,0:T(8,128)(2,1)} %constant.22.clone.refs_1_, bf16[2,128,2304]{2,1,0:T(8,128)(2,1)} %refs_2_.1, bf16[2,128,2048]{2,1,0:T(8,128)(2,1)} %refs_3_.1, ...), custom_call_target="tpu_custom_call" | custom-call | flops 6000000000 | bytes 16000000 | tf_op jit(solution)/shard_map/pallas_call | solution.py:595
  54.0 2.0 %shard_map.168 = (bf16[2,1,128,2048]{3,2,1,0:T(8,128)(2,1)}, f32[57,57]{1,0:T(8,128)}) custom-call(bf16[2,1,128,2048]{3,2,1,0:T(8,128)(2,1)} %get-tuple-element.4.wave_in, f32[57,57]{1,0:T(8,128)} %get-tuple-element.5.kgrad_in), custom_call_target="tpu_custom_call" | custom-call | tf_op jit(solution)/shard_map/pallas_call | solution.py:606
